TPU v7x, 128 devices: a whole 4x4x4 slice. The times are simulated.
128 devices in a mesh: dp: 4 (over y_hi, core), wide: 32 (over z, x, y_lo).
Axes of the slice: x: 4, y: 4 (y_hi: 2, y_lo: 2; y = y_hi * 2 + y_lo), z: 4, core: 2. Of those that a mesh axis runs over, the one named last changes fastest.
Arguments:
- frames: bfloat16 [4, 2, 64, 64, 512], P('dp', None, 'wide'), may hold values from -6 to 6
- conv_weight: bfloat16 [3, 512, 512], replicated, may hold values from -0.15625 to 0.15625
- embed_weight: bfloat16 [512, 1536], replicated, may hold values from -0.25 to 0.25
- query_weight: bfloat16 [1536, 1536], P('wide'), may hold values from -3 to 3
- key_weight: bfloat16 [1536, 1536], P('wide'), may hold values from -3 to 3
- value_weight: bfloat16 [1536, 1536], P('wide'), may hold values from -0.15625 to 0.15625
- output_weight: bfloat16 [1536, 1536], P('wide'), may hold values from -0.15625 to 0.15625
- out_grad: bfloat16 [4, 4, 64, 64, 1536], P('dp', None, 'wide'), may hold values from -0.119628906 to 0.119628906
- bucket_owner: int32 [16], replicated, may hold values from 0 to 3, as said below
- clip_bucket: int32 [4, 2], replicated, may hold values from 0 to 15, as said below
- clip_frames: int32 [4, 2], replicated, may hold values from 16 to 64, as said below
- clip_grid: int32 [4, 2, 2], replicated, may hold values from 2 to 32, as said below
Outputs:
- block_out: bfloat16 [4, 4, 64, 64, 1536], P('dp', None, 'wide')
- grad_query: float32 [1536, 1536], P('wide')
- grad_key: float32 [1536, 1536], P('wide')
- grad_value: float32 [1536, 1536], P('wide')
- grad_output: float32 [1536, 1536], P('wide')
Inputs may be any that keep to these rules, and one draw needn't show every extreme that they name: `bucket_owner`: each owner has exactly 4 buckets. `clip_bucket`: the 2 clips of one group have buckets of different owners; some owner has a clip of every group. `clip_frames`: some clip has all 64 frames. `clip_grid`: the product of a clip's two entries is at most 64, and equals it for some clip.
All inputs are finite; a program needn't handle non-finite values.
Results may differ from a plain program's by a relative error of at most 0.025.
Values may be sent and summed in bfloat16 or wider, within the bound.
No kernel may reach another device: no remote copies, remote signals or barrier semaphores. Data moves between devices by JAX's collectives and lax.ppermute only.
A program may use at most 128 MiB of HBM per device.

v0:
```python
import functools
import math

import jax
import jax.numpy as jnp
from jax import lax
from jax.experimental import pallas as pl
from jax.experimental.pallas import tpu as pltpu
from jax.sharding import PartitionSpec as P

HEAD_DIM = 128
EPS = 1e-06
masked_score = -1e30

NO_COST = pl.CostEstimate(flops=0, bytes_accessed=0, transcendentals=0)

ANYWHERE = pl.BlockSpec(memory_space=pl.ANY)

AXES = ("dp", "wide")
N_DEV = 128
N_WIDE = 32
HEAD_COLS = 384
UNIT_ROWS = 128
UNITS = 2
ROWS = 48


def place_of(index):
    dp, wide = divmod(index, N_WIDE)
    y_hi, core = divmod(dp, 2)
    z, rest = divmod(wide, 8)
    x, y_lo = divmod(rest, 2)
    return core, x, y_hi * 2 + y_lo, z


def index_of(core, x, y, z):
    y_hi, y_lo = divmod(y % 4, 2)
    return (y_hi * 2 + core % 2) * N_WIDE + (z % 4) * 8 + (x % 4) * 2 + y_lo


def pairs_by(move):
    return [(i, index_of(*move(*place_of(i)))) for i in range(N_DEV)]


Y_PARTNER = pairs_by(lambda core, x, y, z: (core, x, y ^ 1, z))
CORE_PARTNER = pairs_by(lambda core, x, y, z: (core ^ 1, x, y, z))
Y_NEXT = pairs_by(lambda core, x, y, z: (core, x, y + 1, z))
Y_BEFORE = pairs_by(lambda core, x, y, z: (core, x, y - 1, z))
Y_ACROSS = pairs_by(lambda core, x, y, z: (core, x, y + 2, z))
DP_MOVES = [[(i, i ^ (k * N_WIDE)) for i in range(N_DEV)] for k in range(4)]
HALO = [(i, i + 1) for i in range(N_DEV) if (i + 1) % N_WIDE]


def output_source(core, x, y, z, flip):
    y_hi, y_lo = divmod(y, 2)
    place, across = (z, x) if core else (x, z)
    return index_of(across // 2, place, y_hi * 2 + ((across % 2) ^ flip), 2 * y_lo + core)


RING_FLIPS = [
    pairs_by(lambda core, x, y, z, k=k: (core, x, y, z ^ k) if core else (core, x ^ k, y, z))
    for k in range(4)
]


OUT_PAIRS = [[(output_source(*place_of(i), flip), i) for i in range(N_DEV)] for flip in (0, 1)]
def spot(index):
    core, x, _, z = place_of(index)
    return z if core else x


def output_target(core, x, y, z, block):
    y_hi, y_lo = divmod(y, 2)
    place, column = (x, z) if core else (z, x)
    return index_of(column // 2, place, y_hi * 2 + block, 2 * y_lo + core)


OUT_BACK = [
    [(i, output_target(*place_of(i), block=(spot(i) % 2) ^ flip)) for i in range(N_DEV)]
    for flip in (0, 1)
]


def rings(axis_of_core):
    groups = []
    for core in range(2):
        for a in range(4):
            for y in range(4):
                if axis_of_core[core] == "z":
                    groups.append([index_of(core, a, y, z) for z in range(4)])
                else:
                    groups.append([index_of(core, x, y, a) for x in range(4)])
    return groups


RINGS_FIRST = rings("xz")
RINGS_SECOND = rings("zx")


def send(array, pairs):
    return lax.ppermute(array, AXES, pairs)


def exchange(array, groups):
    return lax.all_to_all(array, AXES, 0, 0, tiled=True, axis_index_groups=groups)


def spread(array):
    return jnp.broadcast_to(array[None], (4,) + array.shape)


def in_order(bit, mine, other, axis=0):
    return jnp.stack([jnp.where(bit == 0, mine, other), jnp.where(bit == 0, other, mine)], axis)


def after(value, *others):
    return lax.optimization_barrier((value,) + others)[0]


def embed_kernel(rows_ref, weight_ref, out_ref):
    values = dot(rows_ref[...], weight_ref[...]).astype(jnp.bfloat16)
    out_ref[...] = layer_norm(values)


def embed_and_norm(rows, weight):
    tile = 256
    return pl.pallas_call(
        embed_kernel,
        grid=(rows.shape[0] // tile,),
        in_specs=[
            pl.BlockSpec((tile, rows.shape[1]), lambda i: (i, 0)),
            pl.BlockSpec(weight.shape, lambda i: (0, 0)),
        ],
        out_specs=pl.BlockSpec((tile, weight.shape[1]), lambda i: (i, 0)),
        out_shape=jax.ShapeDtypeStruct((rows.shape[0], weight.shape[1]), jnp.bfloat16),
        compiler_params=pltpu.CompilerParams(vmem_limit_bytes=32 * 1024 * 1024),
        cost_estimate=NO_COST,
    )(rows, weight)


def layer_norm(values):
    floats = values.astype(jnp.float32)
    center = floats - jnp.mean(floats, axis=-1, keepdims=True)
    spread = jnp.mean(center * center, axis=-1, keepdims=True)
    return (center * lax.rsqrt(spread + EPS)).astype(jnp.bfloat16)


def dot(a, b, dims=((1,), (0,))):
    return lax.dot_general(a, b, (dims, ((), ())), preferred_element_type=jnp.float32)


def product_kernel(dims, added, a_ref, b_ref, *rest):
    product = dot(a_ref[...], b_ref[...], dims)
    if added:
        product = product + rest[0][...].astype(jnp.float32)
    rest[-1][...] = product.astype(jnp.bfloat16)


def matmul(a, b, dims=(1, 0), tile=256, add=None, others=()):
    rows, depth = a.shape[1 - dims[0]], a.shape[dims[0]]
    columns = b.shape[1 - dims[1]]
    if dims[0]:
        a_spec = pl.BlockSpec((tile, depth), lambda i: (i, 0))
    else:
        a_spec = pl.BlockSpec((depth, tile), lambda i: (0, i))
    out_spec = pl.BlockSpec((tile, columns), lambda i: (i, 0))
    return pl.pallas_call(
        functools.partial(product_kernel, ((dims[0],), (dims[1],)), add is not None),
        grid=(rows // tile,),
        in_specs=[a_spec, pl.BlockSpec(b.shape, lambda i: (0, 0))]
        + ([out_spec] if add is not None else [])
        + [ANYWHERE] * len(others),
        out_specs=out_spec,
        out_shape=jax.ShapeDtypeStruct((rows, columns), jnp.bfloat16),
        compiler_params=pltpu.CompilerParams(vmem_limit_bytes=40 * 1024 * 1024),
        cost_estimate=NO_COST,
    )(*((a, b) if add is None else (a, b, add)), *others)


def matmul_columns(a, b):
    rows, depth = a.shape
    return pl.pallas_call(
        functools.partial(product_kernel, ((1,), (0,)), False),
        grid=(3,),
        in_specs=[
            pl.BlockSpec((rows, depth), lambda i: (0, 0)),
            pl.BlockSpec((depth, HEAD_COLS), lambda i: (0, i)),
        ],
        out_specs=pl.BlockSpec((rows, HEAD_COLS), lambda i: (0, i)),
        out_shape=jax.ShapeDtypeStruct((rows, b.shape[1]), jnp.bfloat16),
        compiler_params=pltpu.CompilerParams(vmem_limit_bytes=40 * 1024 * 1024),
        cost_estimate=NO_COST,
    )(a, b)


def split_kernel(ring_ref, spread_ref, out_ref):
    spread_ref[0] = ring_ref[:, : 3 * HEAD_COLS]

    @pl.when(pl.program_id(0) == 0)
    def _():
        out_ref[...] = ring_ref[:, 3 * HEAD_COLS :]


def split_ring(ring):
    rows, width = ring.shape[0], ring.shape[1] - 3 * HEAD_COLS
    return pl.pallas_call(
        split_kernel,
        grid=(4,),
        in_specs=[pl.BlockSpec(ring.shape, lambda i: (0, 0))],
        out_specs=[
            pl.BlockSpec((1, rows, 3 * HEAD_COLS), lambda i: (i, 0, 0)),
            pl.BlockSpec((rows, width), lambda i: (0, 0)),
        ],
        out_shape=[
            pltpu.HBM((4, rows, 3 * HEAD_COLS), jnp.bfloat16),
            jax.ShapeDtypeStruct((rows, width), jnp.bfloat16),
        ],
        compiler_params=pltpu.CompilerParams(vmem_limit_bytes=32 * 1024 * 1024),
        cost_estimate=NO_COST,
    )(ring)


def term_kernel(normed_ref, d_qkv_ref, att_ref, up_ref, out_ref, total_ref):
    out_ref[0, :, : 3 * HEAD_COLS] = dot(
        normed_ref[...], d_qkv_ref[...], ((0,), (0,))
    ).astype(jnp.bfloat16)

    @pl.when(pl.program_id(0) == 0)
    def _():
        total_ref[...] = dot(att_ref[...], up_ref[...], ((0,), (0,))).astype(jnp.bfloat16)

    at = pl.multiple_of(pl.program_id(0) * 2 * ROWS, 2 * ROWS)
    for block in range(4):
        out_ref[0, block * 2 * ROWS : (block + 1) * 2 * ROWS, 3 * HEAD_COLS :] = total_ref[
            pl.ds(at, 2 * ROWS), block * HEAD_COLS : (block + 1) * HEAD_COLS
        ]


def terms(normed, d_qkv, attended, upstream):
    depth, width = normed.shape
    rows = width // 4
    whole = lambda array: pl.BlockSpec(array.shape, lambda i: (0, 0))
    return pl.pallas_call(
        term_kernel,
        grid=(4,),
        in_specs=[
            pl.BlockSpec((depth, rows), lambda i: (0, i)),
            whole(d_qkv),
            whole(attended),
            whole(upstream),
        ],
        out_specs=pl.BlockSpec((1, rows, 4 * HEAD_COLS), lambda i: (i, 0, 0)),
        out_shape=pltpu.HBM((4, rows, 4 * HEAD_COLS), jnp.bfloat16),
        scratch_shapes=[pltpu.VMEM((HEAD_COLS, width), jnp.bfloat16)],
        compiler_params=pltpu.CompilerParams(vmem_limit_bytes=40 * 1024 * 1024),
        cost_estimate=NO_COST,
    )(normed, d_qkv, attended, upstream)


def sum_kernel(parts_ref, *rest):
    out_ref = rest[-1]
    total = parts_ref[0].astype(jnp.float32)
    for i in range(1, 4):
        total = total + parts_ref[i].astype(jnp.float32)
    out_ref[...] = total.astype(jnp.bfloat16)


def sum_parts(parts, *others):
    rows, width = parts.shape[1:]
    tile = 2 * ROWS if rows > 2 * ROWS else ROWS
    return pl.pallas_call(
        sum_kernel,
        grid=(rows // tile,),
        in_specs=[pl.BlockSpec((4, tile, width), lambda i: (0, i, 0))] + [ANYWHERE] * len(others),
        out_specs=pl.BlockSpec((tile, width), lambda i: (i, 0)),
        out_shape=jax.ShapeDtypeStruct((rows, width), jnp.bfloat16),
        compiler_params=pltpu.CompilerParams(vmem_limit_bytes=32 * 1024 * 1024),
        cost_estimate=NO_COST,
    )(parts, *others)


def final_kernel(place_ref, mine_ref, theirs_ref, query_ref, key_ref, value_ref, output_ref):
    core, y_lo = place_ref[0], place_ref[1]
    wide = 3 * HEAD_COLS
    for kind, out in enumerate((query_ref, key_ref, value_ref)):
        for step in range(2):
            at = step * wide + kind * HEAD_COLS
            mine = mine_ref[:, at : at + HEAD_COLS]
            theirs = theirs_ref[:, at : at + HEAD_COLS].astype(jnp.float32)
            low = jnp.where(core == 0, mine, theirs)
            high = jnp.where(core == 0, theirs, mine)
            for side in range(2):

                @pl.when((y_lo ^ step) == side)
                def _():
                    begin = 2 * side * HEAD_COLS
                    out[:, begin : begin + HEAD_COLS] = low
                    out[:, begin + HEAD_COLS : begin + 2 * HEAD_COLS] = high

    mine = mine_ref[:, 2 * wide :]
    theirs = theirs_ref[:, 2 * wide :].astype(jnp.float32)
    output_ref[:, : 2 * HEAD_COLS] = jnp.where(core == 0, mine, theirs)
    output_ref[:, 2 * HEAD_COLS :] = jnp.where(core == 0, theirs, mine)


def final_grads(core, y_lo, mine, theirs):
    rows, width = mine.shape[0], 4 * HEAD_COLS
    whole = pl.BlockSpec(memory_space=pltpu.VMEM)
    return pl.pallas_call(
        final_kernel,
        in_specs=[pl.BlockSpec(memory_space=pltpu.SMEM), whole, whole],
        out_specs=[whole] * 4,
        out_shape=[jax.ShapeDtypeStruct((rows, width), jnp.float32)] * 4,
        cost_estimate=NO_COST,
    )(jnp.stack([core, y_lo]).astype(jnp.int32), mine, theirs)


def attention_kernel(limit_ref, qkv_ref, d_att_ref, att_ref, grads_ref):
    rows = UNIT_ROWS
    sites = rows // 2
    scale = 1.0 / math.sqrt(HEAD_DIM)
    row = lax.broadcasted_iota(jnp.int32, (rows, rows), 0)
    col = lax.broadcasted_iota(jnp.int32, (rows, rows), 1)
    upper = col >= sites
    site = jnp.where(upper, col - sites, col)
    block = upper == (row >= sites)
    masks = [
        block & (site < limit_ref[pl.program_id(0) * UNITS + unit]) for unit in range(UNITS)
    ]
    units = [(unit, head) for unit in range(UNITS) for head in range(HEAD_COLS // HEAD_DIM)]

    def part(ref, unit, head, kind):
        return ref[
            unit * rows : (unit + 1) * rows,
            kind * HEAD_COLS + head * HEAD_DIM : kind * HEAD_COLS + (head + 1) * HEAD_DIM,
        ]

    def put(ref, unit, head, kind, value):
        ref[
            unit * rows : (unit + 1) * rows,
            kind * HEAD_COLS + head * HEAD_DIM : kind * HEAD_COLS + (head + 1) * HEAD_DIM,
        ] = value.astype(jnp.bfloat16)

    scores = [
        dot(part(qkv_ref, u, h, 0), part(qkv_ref, u, h, 1), ((1,), (1,))) for u, h in units
    ]
    d_probs = [
        dot(part(d_att_ref, u, h, 0), part(qkv_ref, u, h, 2), ((1,), (1,))) for u, h in units
    ]
    low = []
    d_scores = []
    for (u, h), score, d_prob in zip(units, scores, d_probs):
        score = jnp.where(masks[u], score * scale, masked_score)
        weights = jnp.exp(score - jnp.max(score, axis=-1, keepdims=True))
        probs = weights * (1.0 / jnp.sum(weights, axis=-1, keepdims=True))
        inner = jnp.sum(probs * d_prob, axis=-1, keepdims=True)
        low.append(probs.astype(jnp.bfloat16))
        d_scores.append((probs * (d_prob - inner) * scale).astype(jnp.bfloat16))
    for (u, h), prob, d_score in zip(units, low, d_scores):
        put(att_ref, u, h, 0, dot(prob, part(qkv_ref, u, h, 2)))
        put(grads_ref, u, h, 0, dot(d_score, part(qkv_ref, u, h, 1)))
        put(grads_ref, u, h, 1, dot(d_score, part(qkv_ref, u, h, 0), ((0,), (0,))))
        put(grads_ref, u, h, 2, dot(prob, part(d_att_ref, u, h, 0), ((0,), (0,))))


def attention(limits, qkv, d_att):
    rows = UNITS * UNIT_ROWS
    count = qkv.shape[0] // rows
    spec = lambda width: pl.BlockSpec((rows, width), lambda i, limits: (i, 0))
    return pl.pallas_call(
        attention_kernel,
        grid_spec=pltpu.PrefetchScalarGridSpec(
            num_scalar_prefetch=1,
            grid=(count,),
            in_specs=[spec(3 * HEAD_COLS), spec(HEAD_COLS)],
            out_specs=[spec(HEAD_COLS), spec(3 * HEAD_COLS)],
        ),
        out_shape=[
            jax.ShapeDtypeStruct((qkv.shape[0], HEAD_COLS), jnp.bfloat16),
            jax.ShapeDtypeStruct((qkv.shape[0], 3 * HEAD_COLS), jnp.bfloat16),
        ],
        compiler_params=pltpu.CompilerParams(vmem_limit_bytes=32 * 1024 * 1024),
        cost_estimate=NO_COST,
    )(limits, qkv, d_att)


def body(
    frames,
    conv_weight,
    embed_weight,
    query_weight,
    key_weight,
    value_weight,
    output_weight,
    out_grad,
    bucket_owner,
    clip_bucket,
    clip_frames,
    clip_grid,
):
    my_dp = lax.axis_index("dp")
    my_slab = lax.axis_index("wide")
    core, y_hi = my_dp % 2, my_dp // 2
    y_lo = my_slab % 2
    heads_now = 2 * y_lo + core
    heads_across = 2 * (1 - y_lo) + core
    frame_slab = frames[0]
    clip_count, slab_frames, site_count, channels = frame_slab.shape
    width = embed_weight.shape[1]
    own_rows = clip_count * slab_frames * site_count

    def head_columns(which):
        return jnp.concatenate(
            [
                lax.dynamic_slice(w, (0, which * HEAD_COLS), (ROWS, HEAD_COLS))
                for w in (query_weight, key_weight, value_weight)
            ],
            axis=1,
        )

    x_place, z_place = (my_slab // 2) % 4, my_slab // 8
    place = jnp.where(core == 0, x_place, z_place)
    across_place = jnp.where(core == 0, z_place, x_place)
    parity = across_place % 2

    outgoing = head_columns(heads_across)
    grads, outgoing = lax.optimization_barrier((out_grad[0], outgoing))
    pair = in_order(y_lo, head_columns(heads_now), send(outgoing, Y_PARTNER))
    pair, frame_slab = lax.optimization_barrier((pair, frame_slab))
    out_pair = in_order(
        parity, send(output_weight, OUT_PAIRS[0]), send(output_weight, OUT_PAIRS[1])
    )
    first_operand = spread(jnp.concatenate([pair, out_pair], axis=2))
    embed_weight = after(embed_weight, first_operand)
    earlier = send(frame_slab, HALO)
    bucket_owner, clip_bucket, clip_frames, clip_grid = lax.optimization_barrier(
        (bucket_owner, clip_bucket, clip_frames, clip_grid, earlier)
    )[:-1]
    ring = exchange(first_operand, RINGS_FIRST)
    owners = bucket_owner[clip_bucket]
    tokens = clip_grid[..., 0] * clip_grid[..., 1]
    my_owners = owners[my_dp]
    frame_pos = my_slab * slab_frames + jnp.arange(slab_frames, dtype=jnp.int32)
    site_pos = jnp.arange(site_count, dtype=jnp.int32)
    live = (frame_pos[None, :, None] < clip_frames[my_dp][:, None, None]) & (
        site_pos[None, None, :] < tokens[my_dp][:, None, None]
    )
    group_tokens = lax.dynamic_slice(tokens, (2 * y_hi, 0), (2, clip_count)).reshape(-1)
    limits = jnp.concatenate([group_tokens, group_tokens])

    def to_group(own, *others):
        both = in_order(y_lo, own, after(send(own, Y_PARTNER), *others))
        return in_order(core, both, send(both, CORE_PARTNER), axis=1).reshape(-1, own.shape[-1])

    joined = jnp.concatenate([earlier, frame_slab], axis=1)
    active = jax.nn.silu(joined.astype(jnp.float32)).astype(jnp.bfloat16)
    summed = frame_slab.astype(jnp.float32).reshape(-1, channels)
    for offset in range(3):
        moved = active[:, slab_frames - offset : 2 * slab_frames - offset].reshape(-1, channels)
        summed = summed + dot(moved, conv_weight[offset])
    encoded = summed.astype(jnp.bfloat16)
    own_grouped = dot(encoded, embed_weight).astype(jnp.bfloat16)
    swapped = embed_weight.reshape(channels, 4, 4, -1).swapaxes(1, 2).reshape(channels, width)
    embed_now = jnp.where(core == 0, embed_weight, swapped)

    flips = [my_owners[clip] ^ my_dp for clip in range(clip_count)]
    from_owner = []
    for k in range(4):
        part = lax.dynamic_index_in_dim(grads, my_dp ^ k, 0, keepdims=False)
        part = after(part, first_operand) if k == 1 else part
        from_owner.append(part if k == 0 else send(part, DP_MOVES[k]))
    to_them = [
        jnp.where(flips[0] == k, 0, jnp.where(flips[1] == k, 1, 2)).astype(jnp.int32)
        for k in range(4)
    ]
    ring, embed_now, limits, *to_them = lax.optimization_barrier(
        (ring, embed_now, limits, *to_them)
    )
    from_owner = [after(part, ring) for part in from_owner]
    clip_up = []
    for clip in range(clip_count):
        flip = flips[clip]
        low = jnp.where(flip == 0, from_owner[0], from_owner[1])
        high = jnp.where(flip == 2, from_owner[2], from_owner[3])
        clip_up.append(jnp.where(flip < 2, low, high))
    own_up = jnp.where(live[..., None], jnp.stack(clip_up), jnp.zeros((), jnp.bfloat16))
    own_up = own_up.reshape(own_rows, width)
    second_operand, out_rows = split_ring(ring.reshape(8 * ROWS, -1))
    qkv_weight = exchange(second_operand, RINGS_SECOND).reshape(width, 3 * HEAD_COLS)

    normed = embed_and_norm(to_group(encoded, ring), embed_now)
    upstream = to_group(own_up, qkv_weight, normed)

    qkv = matmul_columns(normed, qkv_weight)
    d_attended = matmul(upstream, out_rows, (1, 1))
    attended, d_qkv = attention(limits, qkv, d_attended)

    term = terms(normed, d_qkv, attended, upstream)
    attended, term = lax.optimization_barrier((attended, term))
    by_core = attended.reshape(2, 2, own_rows, HEAD_COLS)
    rows_now, rows_across = (
        lax.dynamic_index_in_dim(by_core, which, 1, keepdims=False).reshape(-1, HEAD_COLS)
        for which in (core, 1 - core)
    )
    give_core = send(matmul(rows_across, out_rows), CORE_PARTNER)
    chip = matmul(rows_now, out_rows, add=give_core).reshape(2, own_rows, width)
    give_y = lax.dynamic_index_in_dim(chip, 1 - y_lo, 0, keepdims=False)

    keep = lax.dynamic_index_in_dim(chip, y_lo, 0, keepdims=False)
    projected = keep.astype(jnp.float32) + send(give_y, Y_PARTNER).astype(jnp.float32)
    block = (own_grouped.astype(jnp.float32) + projected).astype(jnp.bfloat16)
    block = block.reshape(clip_count, slab_frames, site_count, width)
    block = jnp.where(live[..., None], block, jnp.zeros((), jnp.bfloat16))
    block = jnp.concatenate([block, jnp.zeros_like(block[:1])])

    arrived, sent = [], []
    for k in range(4):
        part = lax.dynamic_index_in_dim(block, to_them[k], 0, keepdims=False)
        sent.append(part)
        arrived.append(part if k == 0 else send(part, DP_MOVES[k]))

    def reduced(array, groups, *others):
        return sum_parts(exchange(array, groups), *others)

    first_sum = reduced(term, RINGS_SECOND, *sent[1:])
    part = reduced(first_sum.reshape(4, 2 * ROWS, -1), RINGS_FIRST)
    part = part.reshape(2, ROWS, -1)
    part_qkv, part_out = part[..., : 3 * HEAD_COLS], part[..., 3 * HEAD_COLS :]
    even, odd = (
        lax.dynamic_index_in_dim(part_out, which, 0, keepdims=False)
        for which in (place % 2, 1 - place % 2)
    )
    came = in_order(y_lo, send(even, OUT_BACK[0]), send(odd, OUT_BACK[1]))
    mine_out = jnp.concatenate([came[0], came[1]], axis=1)
    mine_qkv = lax.dynamic_index_in_dim(part_qkv, y_lo, 0, keepdims=False)
    other_qkv = lax.dynamic_index_in_dim(part_qkv, 1 - y_lo, 0, keepdims=False)
    across = send(mine_qkv, Y_ACROSS).astype(jnp.float32)
    behind = send(other_qkv, Y_NEXT).astype(jnp.float32)
    before = send(other_qkv, Y_BEFORE).astype(jnp.float32)
    same = mine_qkv.astype(jnp.float32) + across
    cross = behind + before
    sums = jnp.concatenate([same, cross], axis=1)
    across = after(send(mine_out, Y_ACROSS), sums).astype(jnp.float32)
    mine = jnp.concatenate([sums, mine_out.astype(jnp.float32) + across], axis=1)
    theirs = send(mine.astype(jnp.bfloat16), CORE_PARTNER)
    grad_query, grad_key, grad_value, grad_output = final_grads(core, y_lo, mine, theirs)

    a0, a1, a2, a3 = (after(part, sums) for part in arrived)
    a0, a1 = jnp.where(core == 0, a0, a1), jnp.where(core == 0, a1, a0)
    a2, a3 = jnp.where(core == 0, a2, a3), jnp.where(core == 0, a3, a2)
    first, second = jnp.stack([a0, a1]), jnp.stack([a2, a3])
    block_out = in_order(y_hi, first, second).reshape(
        1, 4, slab_frames, site_count, width
    )
    return (block_out, grad_query, grad_key, grad_value, grad_output)


def solution(mesh):
    in_specs = (
        P("dp", None, "wide", None, None),
        P(),
        P(),
        P("wide", None),
        P("wide", None),
        P("wide", None),
        P("wide", None),
        P("dp", None, "wide", None, None),
        P(),
        P(),
        P(),
        P(),
    )
    out_specs = (
        P("dp", None, "wide", None, None),
        P("wide", None),
        P("wide", None),
        P("wide", None),
        P("wide", None),
    )
    return jax.shard_map(body, mesh=mesh, in_specs=in_specs, out_specs=out_specs, check_vma=False)
```

profile of v0, /device:TPU:3, one launch (start us, length us, event | category | flops | bytes accessed | tf_op | source)
XLA Modules:
  0.0 197.0 jit_solution(8273704279373292286)
XLA Ops:
  0.6 6.1 %collective-permute-start.2 = (bf16[48,1536]{1,0:T(8,128)(2,1)}, bf16[48,1536]{1,0:T(8,128)(2,1)S(1)}, u32[]{:S(2)}, u32[]{:S(2)}) collective-permute-start(bf16[48,1536]{1,0:T(8,128)(2,1)} %param.18), channel_id=1, source_target_pairs={{0,0},{16,1},{2,2},{18,3},{4,4},{20,5},{6,6},{22,7},{1,8},{17,9},{... | collective-permute-start | bytes 442376 | tf_op jit(solution)/shard_map/ppermute | solution.py:101
  13.6 2.6 %collective-permute-start.7 = (bf16[2,64,1536]{2,1,0:T(8,128)(2,1)}, bf16[2,64,1536]{2,1,0:T(8,128)(2,1)}, u32[]{:S(2)}, u32[]{:S(2)}) collective-permute-start(bf16[2,64,1536]{2,1,0:T(8,128)(2,1)} %get-tuple-element.91), channel_id=1, source_target_pairs={{0,64},{1,65},{2,66},{3,67},{4,68},{5,69},{6,70},{7,71},{8,72},{9,... | collective-permute-start | bytes 1179656 | tf_op jit(solution)/shard_map/ppermute | solution.py:101
  20.8 5.2 %all-to-all-start = ((bf16[4,2,48,2688]{3,2,1,0:T(8,128)(2,1)}), bf16[4,2,48,2688]{3,2,1,0:T(8,128)(2,1)S(1)}, u32[]{:S(2)}, u32[]{:S(2)}) async-start(bf16[4,2,48,2688]{3,2,1,0:T(8,128)(2,1)} %broadcast_in_dim.35), calls=%async_computation | async-start | bytes 4128768 | tf_op jit(solution)/shard_map/all_to_all | solution.py:105
  26.0 2.6 %copy.24 = bf16[512,1536]{0,1:T(8,128)(2,1)} copy(bf16[512,1536]{1,0:T(8,128)(2,1)} %param.14) | data formatting | bytes 3145728 | tf_op jit(solution)/shard_map/optimization_barrier | solution.py:117
  28.5 2.7 %copy.25 = bf16[512,4,4,96]{0,3,2,1:T(8,128)(2,1)} copy(bf16[512,4,4,96]{0,3,1,2:T(8,128)(2,1)} %bitcast.130) | data formatting | bytes 3145728 | tf_op jit(solution)/shard_map/transpose | solution.py:463
  31.2 2.6 %copy.26 = bf16[512,1536]{1,0:T(8,128)(2,1)} copy(bf16[512,1536]{0,1:T(8,128)(2,1)} %bitcast.129) | data formatting | bytes 3145728 | tf_op jit(solution)/shard_map/reshape | solution.py:463
  33.8 2.7 %broadcast_select_fusion.weight_ref = bf16[512,1536]{1,0:T(8,128)(2,1)} fusion(bf16[512,1536]{1,0:T(8,128)(2,1)} %param.14, bf16[512,1536]{1,0:T(8,128)(2,1)} %copy.26, pred[]{:T(512)S(6)} %eq.32), kind=kLoop, calls=%fused_computation.11 | loop fusion | flops 786432 | bytes 4718593 | tf_op jit(solution)/shard_map/jit(_where)/select_n | solution.py:464
  50.1 5.0 %all-to-all-start.1 = ((bf16[4,384,1152]{2,1,0:T(8,128)(2,1)}), bf16[4,384,1152]{2,1,0:T(8,128)(2,1)}, u32[]{:S(2)}, u32[]{:S(2)}) async-start(bf16[4,384,1152]{2,1,0:T(8,128)(2,1)} %get-tuple-element.55), calls=%async_computation.1 | async-start | bytes 7077888 | tf_op jit(solution)/shard_map/all_to_all | solution.py:105
  59.3 3.8 %shard_map.155.a_ref.normed_ref = bf16[1024,1536]{1,0:T(8,128)(2,1)S(1)} custom-call(bf16[1024,512]{1,0:T(8,128)(2,1)S(1)} %bitcast.123, bf16[512,1536]{1,0:T(8,128)(2,1)S(1)} %copy-done.5), custom_call_target="tpu_custom_call" | custom-call | tf_op jit(solution)/shard_map/pallas_call | solution.py:127
  63.1 12.8 %collective-permute-done.9 = bf16[256,1536]{1,0:T(8,128)(2,1)} collective-permute-done((bf16[256,1536]{1,0:T(8,128)(2,1)S(1)}, bf16[256,1536]{1,0:T(8,128)(2,1)}, u32[]{:S(2)}, u32[]{:S(2)}) %collective-permute-start.9) | collective-permute-done | bytes 786464 | tf_op jit(solution)/shard_map/ppermute | solution.py:101
  82.7 7.0 %shard_map.157.qkv_ref = bf16[1024,1152]{1,0:T(8,128)(2,1)S(1)} custom-call(bf16[1024,1536]{1,0:T(8,128)(2,1)S(1)} %shard_map.155.a_ref.normed_ref, bf16[1536,1152]{1,0:T(8,128)(2,1)} %bitcast.24.b_ref), custom_call_target="tpu_custom_call" | custom-call | tf_op jit(solution)/shard_map/pallas_call | solution.py:182
  95.2 4.4 %shard_map.159 = (bf16[1024,384]{1,0:T(8,128)(2,1)S(1)}, bf16[1024,1152]{1,0:T(8,128)(2,1)S(1)}) custom-call(s32[8]{0:T(128)S(1)} %pad_add_fusion.limit_ref, bf16[1024,1152]{1,0:T(8,128)(2,1)S(1)} %shard_map.157.qkv_ref, bf16[1024,384]{1,0:T(8,128)(2,1)S(1)} %shard_map.158.d_att_ref), custom_call_target="tpu_custom_call" | custom-call | tf_op jit(solution)/shard_map/pallas_call | solution.py:370
  99.6 7.9 %shard_map.160 = bf16[4,384,1536]{2,1,0:T(8,128)(2,1)} custom-call(bf16[1024,1536]{1,0:T(8,128)(2,1)S(1)} %shard_map.155.a_ref.normed_ref, bf16[1024,1152]{1,0:T(8,128)(2,1)S(1)} %get-tuple-element.65.d_qkv_ref, bf16[1024,384]{1,0:T(8,128)(2,1)S(1)} %get-tuple-element.66.att_ref, bf16[1024,1536]{1,0:T(8,128)(2,1)S(1)} %bitcast.119), custom_call_target="tpu_custom_call" | custom-call | tf_op jit(solution)/shard_map/pallas_call | solution.py:243
  108.9 6.7 %all-to-all-start.2 = ((bf16[4,384,1536]{2,1,0:T(8,128)(2,1)}), bf16[4,384,1536]{2,1,0:T(8,128)(2,1)}, u32[]{:S(2)}, u32[]{:S(2)}) async-start(bf16[4,384,1536]{2,1,0:T(8,128)(2,1)} %shard_map.160), calls=%async_computation.2 | async-start | bytes 9437184 | tf_op jit(solution)/shard_map/all_to_all | solution.py:105
  121.3 16.7 %collective-permute-done.12 = bf16[256,1536]{1,0:T(8,128)(2,1)} collective-permute-done((bf16[256,1536]{1,0:T(8,128)(2,1)}, bf16[256,1536]{1,0:T(8,128)(2,1)}, u32[]{:S(2)}, u32[]{:S(2)}) %collective-permute-start.12) | collective-permute-done | bytes 786464 | tf_op jit(solution)/shard_map/ppermute | solution.py:101
  140.3 3.9 %all-to-all-done.2.parts_ref = bf16[4,384,1536]{2,1,0:T(8,128)(2,1)} async-done(((bf16[4,384,1536]{2,1,0:T(8,128)(2,1)}), bf16[4,384,1536]{2,1,0:T(8,128)(2,1)}, u32[]{:S(2)}, u32[]{:S(2)}) %all-to-all-start.2) | async-done | bytes 4718624 | tf_op jit(solution)/shard_map/all_to_all | solution.py:105
  144.2 4.3 %shard_map.163 = bf16[384,1536]{1,0:T(8,128)(2,1)} custom-call(bf16[4,384,1536]{2,1,0:T(8,128)(2,1)} %all-to-all-done.2.parts_ref, bf16[2,64,1536]{2,1,0:T(8,128)(2,1)S(1)} %get-tuple-element.98.rest_0_, bf16[2,64,1536]{2,1,0:T(8,128)(2,1)S(1)} %get-tuple-element.99.rest_1_, bf16[2,64,1536]{2,1,0:T(8,128)(2,1)S(1)} %get-tuple-element.100.rest_2_), custom_call_target="tpu_custom_call" | custom-call | tf_op jit(solution)/shard_map/pallas_call | solution.py:271
  148.5 3.6 %all-to-all-start.3 = ((bf16[4,96,1536]{2,1,0:T(8,128)(2,1)}), bf16[4,96,1536]{2,1,0:T(8,128)(2,1)S(1)}, u32[]{:S(2)}, u32[]{:S(2)}) async-start(bf16[4,96,1536]{2,1,0:T(8,128)(2,1)} %bitcast.49), calls=%async_computation.3 | async-start | bytes 2359296 | tf_op jit(solution)/shard_map/all_to_all | solution.py:105
  152.7 2.6 %collective-permute-start.16 = (bf16[2,64,1536]{2,1,0:T(8,128)(2,1)S(1)}, bf16[2,64,1536]{2,1,0:T(8,128)(2,1)S(1)}, u32[]{:S(2)}, u32[]{:S(2)}) collective-permute-start(bf16[2,64,1536]{2,1,0:T(8,128)(2,1)S(1)} %get-tuple-element.98.rest_0_), channel_id=1, source_target_pairs={{0,32},{1,33},{2,34},{3,35},{4,36},{5,37},{6,38},{7,39},{8,40},{9,... | collective-permute-start | bytes 1179656 | tf_op jit(solution)/shard_map/ppermute | solution.py:101
  158.2 4.6 %all-to-all-done.3.parts_ref = bf16[4,96,1536]{2,1,0:T(8,128)(2,1)S(1)} async-done(((bf16[4,96,1536]{2,1,0:T(8,128)(2,1)}), bf16[4,96,1536]{2,1,0:T(8,128)(2,1)S(1)}, u32[]{:S(2)}, u32[]{:S(2)}) %all-to-all-start.3) | async-done | bytes 1179680 | tf_op jit(solution)/shard_map/all_to_all | solution.py:105
  163.1 4.1 %collective-permute-start.19 = (bf16[48,384]{1,0:T(8,128)(2,1)S(1)}, bf16[48,384]{1,0:T(8,128)(2,1)S(1)}, u32[]{:S(2)}, u32[]{:S(2)}) collective-permute-start(bf16[48,384]{1,0:T(8,128)(2,1)S(1)} %get-tuple-element.124), channel_id=1, source_target_pairs={{0,0},{1,16},{2,1},{3,17},{4,32},{5,48},{6,33},{7,49},{8,2},{9,18}... | collective-permute-start | bytes 110600 | tf_op jit(solution)/shard_map/ppermute | solution.py:101
  171.4 4.0 %collective-permute-done.20 = bf16[48,384]{1,0:T(8,128)(2,1)S(1)} collective-permute-done((bf16[48,384]{1,0:T(8,128)(2,1)S(1)}, bf16[48,384]{1,0:T(8,128)(2,1)S(1)}, u32[]{:S(2)}, u32[]{:S(2)}) %collective-permute-start.20) | collective-permute-done | bytes 36896 | tf_op jit(solution)/shard_map/ppermute | solution.py:101
  175.5 3.4 %collective-permute-done.13 = bf16[48,1152]{1,0:T(8,128)(2,1)S(1)} collective-permute-done((bf16[48,1152]{1,0:T(8,128)(2,1)S(1)}, bf16[48,1152]{1,0:T(8,128)(2,1)S(1)}, u32[]{:S(2)}, u32[]{:S(2)}) %collective-permute-start.13) | collective-permute-done | bytes 110624 | tf_op jit(solution)/shard_map/ppermute | solution.py:101
  186.0 6.8 %collective-permute-start.22 = (bf16[48,3072]{1,0:T(8,128)(2,1)S(1)}, bf16[48,3072]{1,0:T(8,128)(2,1)S(1)}, u32[]{:S(2)}, u32[]{:S(2)}) collective-permute-start(bf16[48,3072]{1,0:T(8,128)(2,1)S(1)} %fusion.20), channel_id=1, source_target_pairs={{0,32},{1,33},{2,34},{3,35},{4,36},{5,37},{6,38},{7,39},{8,40},{9,... | collective-permute-start | bytes 884744 | tf_op jit(solution)/shard_map/ppermute | solution.py:101
  (149 shorter events, 68.5 us)
Async XLA Ops:
  0.6 18.6 %collective-permute-start.2 = (bf16[48,1536]{1,0:T(8,128)(2,1)}, bf16[48,1536]{1,0:T(8,128)(2,1)S(1)}, u32[]{:S(2)}, u32[]{:S(2)}) collective-permute-start(bf16[48,1536]{1,0:T(8,128)(2,1)} %param.18), channel_id=1, source_target_pairs={{0,0},{16,1},{2,2},{18,3},{4,4},{20,5},{6,6},{22,7},{1,8},{17,9},{... | collective-permute-start | bytes 442376 | tf_op jit(solution)/shard_map/ppermute | solution.py:101
  6.7 12.5 %collective-permute-start.3 = (bf16[48,1536]{1,0:T(8,128)(2,1)}, bf16[48,1536]{1,0:T(8,128)(2,1)S(1)}, u32[]{:S(2)}, u32[]{:S(2)}) collective-permute-start(bf16[48,1536]{1,0:T(8,128)(2,1)} %param.18), channel_id=1, source_target_pairs={{1,0},{17,1},{3,2},{19,3},{5,4},{21,5},{7,6},{23,7},{0,8},{16,9},{... | collective-permute-start | bytes 442376 | tf_op jit(solution)/shard_map/ppermute | solution.py:101
  10.3 6.9 %collective-permute-start = (bf16[48,1152]{1,0:T(8,128)(2,1)S(1)}, bf16[48,1152]{1,0:T(8,128)(2,1)S(1)}, u32[]{:S(2)}, u32[]{:S(2)}) collective-permute-start(bf16[48,1152]{1,0:T(8,128)(2,1)S(1)} %pad_maximum_fusion.12), channel_id=1, source_target_pairs={{0,1},{1,0},{2,3},{3,2},{4,5},{5,4},{6,7},{7,6},{8,9},{9,8},{10,11... | collective-permute-start | bytes 331784 | tf_op jit(solution)/shard_map/ppermute | solution.py:101
  13.6 41.5 %collective-permute-start.7 = (bf16[2,64,1536]{2,1,0:T(8,128)(2,1)}, bf16[2,64,1536]{2,1,0:T(8,128)(2,1)}, u32[]{:S(2)}, u32[]{:S(2)}) collective-permute-start(bf16[2,64,1536]{2,1,0:T(8,128)(2,1)} %get-tuple-element.91), channel_id=1, source_target_pairs={{0,64},{1,65},{2,66},{3,67},{4,68},{5,69},{6,70},{7,71},{8,72},{9,... | collective-permute-start | bytes 1179656 | tf_op jit(solution)/shard_map/ppermute | solution.py:101
  16.3 38.9 %collective-permute-start.8 = (bf16[2,64,1536]{2,1,0:T(8,128)(2,1)}, bf16[2,64,1536]{2,1,0:T(8,128)(2,1)}, u32[]{:S(2)}, u32[]{:S(2)}) collective-permute-start(bf16[2,64,1536]{2,1,0:T(8,128)(2,1)} %get-tuple-element.90), channel_id=1, source_target_pairs={{0,96},{1,97},{2,98},{3,99},{4,100},{5,101},{6,102},{7,103},{8,104... | collective-permute-start | bytes 1179656 | tf_op jit(solution)/shard_map/ppermute | solution.py:101
  17.3 21.0 %collective-permute-start.1 = (bf16[2,2,64,512]{3,2,1,0:T(8,128)(2,1)S(1)}, bf16[2,2,64,512]{3,2,1,0:T(8,128)(2,1)S(1)}, u32[]{:S(2)}, u32[]{:S(2)}) collective-permute-start(bf16[2,2,64,512]{3,2,1,0:T(8,128)(2,1)S(1)} %bitcast.135), channel_id=1, source_target_pairs={{0,1},{1,2},{2,3},{3,4},{4,5},{5,6},{6,7},{7,8},{8,9},{9,10},{10,1... | collective-permute-start | bytes 786440 | tf_op jit(solution)/shard_map/ppermute | solution.py:101
  20.8 25.8 %all-to-all-start = ((bf16[4,2,48,2688]{3,2,1,0:T(8,128)(2,1)}), bf16[4,2,48,2688]{3,2,1,0:T(8,128)(2,1)S(1)}, u32[]{:S(2)}, u32[]{:S(2)}) async-start(bf16[4,2,48,2688]{3,2,1,0:T(8,128)(2,1)} %broadcast_in_dim.35), calls=%async_computation | async-start | bytes 4128768 | tf_op jit(solution)/shard_map/all_to_all | solution.py:105
  36.6 18.6 %collective-permute-start.6 = (bf16[2,64,1536]{2,1,0:T(8,128)(2,1)}, bf16[2,64,1536]{2,1,0:T(8,128)(2,1)}, u32[]{:S(2)}, u32[]{:S(2)}) collective-permute-start(bf16[2,64,1536]{2,1,0:T(8,128)(2,1)} %get-tuple-element.58), channel_id=1, source_target_pairs={{0,32},{1,33},{2,34},{3,35},{4,36},{5,37},{6,38},{7,39},{8,40},{9,... | collective-permute-start | bytes 1179656 | tf_op jit(solution)/shard_map/ppermute | solution.py:101
  41.6 13.6 %collective-permute-start.4 = (bf16[256,512]{1,0:T(8,128)(2,1)S(1)}, bf16[256,512]{1,0:T(8,128)(2,1)S(1)}, u32[]{:S(2)}, u32[]{:S(2)}) collective-permute-start(bf16[256,512]{1,0:T(8,128)(2,1)S(1)} %fusion.3), channel_id=1, source_target_pairs={{0,1},{1,0},{2,3},{3,2},{4,5},{5,4},{6,7},{7,6},{8,9},{9,8},{10,11... | collective-permute-start | bytes 786440 | tf_op jit(solution)/shard_map/ppermute | solution.py:101
  50.1 27.8 %all-to-all-start.1 = ((bf16[4,384,1152]{2,1,0:T(8,128)(2,1)}), bf16[4,384,1152]{2,1,0:T(8,128)(2,1)}, u32[]{:S(2)}, u32[]{:S(2)}) async-start(bf16[4,384,1152]{2,1,0:T(8,128)(2,1)} %get-tuple-element.55), calls=%async_computation.1 | async-start | bytes 7077888 | tf_op jit(solution)/shard_map/all_to_all | solution.py:105
  57.1 18.8 %collective-permute-start.9 = (bf16[256,1536]{1,0:T(8,128)(2,1)S(1)}, bf16[256,1536]{1,0:T(8,128)(2,1)}, u32[]{:S(2)}, u32[]{:S(2)}) collective-permute-start(bf16[256,1536]{1,0:T(8,128)(2,1)S(1)} %bitcast_select_fusion), channel_id=1, source_target_pairs={{0,1},{1,0},{2,3},{3,2},{4,5},{5,4},{6,7},{7,6},{8,9},{9,8},{10,11... | collective-permute-start | bytes 2359304 | tf_op jit(solution)/shard_map/ppermute | solution.py:101
  81.1 8.5 %collective-permute-start.10 = (bf16[2,256,1536]{2,1,0:T(8,128)(2,1)}, bf16[2,256,1536]{2,1,0:T(8,128)(2,1)}, u32[]{:S(2)}, u32[]{:S(2)}) collective-permute-start(bf16[2,256,1536]{2,1,0:T(8,128)(2,1)} %pad_maximum_fusion.1), channel_id=1, source_target_pairs={{0,32},{1,33},{2,34},{3,35},{4,36},{5,37},{6,38},{7,39},{8,40},{9,... | collective-permute-start | bytes 4718600 | tf_op jit(solution)/shard_map/ppermute | solution.py:101
  108.8 6.8 %collective-permute-start.11 = (bf16[512,1536]{1,0:T(8,128)(2,1)S(1)}, bf16[512,1536]{1,0:T(8,128)(2,1)}, u32[]{:S(2)}, u32[]{:S(2)}) collective-permute-start(bf16[512,1536]{1,0:T(8,128)(2,1)S(1)} %shard_map.161), channel_id=1, source_target_pairs={{0,32},{1,33},{2,34},{3,35},{4,36},{5,37},{6,38},{7,39},{8,40},{9,... | collective-permute-start | bytes 4718600 | tf_op jit(solution)/shard_map/ppermute | solution.py:101
  108.9 35.3 %all-to-all-start.2 = ((bf16[4,384,1536]{2,1,0:T(8,128)(2,1)}), bf16[4,384,1536]{2,1,0:T(8,128)(2,1)}, u32[]{:S(2)}, u32[]{:S(2)}) async-start(bf16[4,384,1536]{2,1,0:T(8,128)(2,1)} %shard_map.160), calls=%async_computation.2 | async-start | bytes 9437184 | tf_op jit(solution)/shard_map/all_to_all | solution.py:105
  118.8 19.2 %collective-permute-start.12 = (bf16[256,1536]{1,0:T(8,128)(2,1)}, bf16[256,1536]{1,0:T(8,128)(2,1)}, u32[]{:S(2)}, u32[]{:S(2)}) collective-permute-start(bf16[256,1536]{1,0:T(8,128)(2,1)} %dynamic-slice_bitcast_fusion), channel_id=1, source_target_pairs={{0,1},{1,0},{2,3},{3,2},{4,5},{5,4},{6,7},{7,6},{8,9},{9,8},{10,11... | collective-permute-start | bytes 2359304 | tf_op jit(solution)/shard_map/ppermute | solution.py:101
  148.5 14.3 %all-to-all-start.3 = ((bf16[4,96,1536]{2,1,0:T(8,128)(2,1)}), bf16[4,96,1536]{2,1,0:T(8,128)(2,1)S(1)}, u32[]{:S(2)}, u32[]{:S(2)}) async-start(bf16[4,96,1536]{2,1,0:T(8,128)(2,1)} %bitcast.49), calls=%async_computation.3 | async-start | bytes 2359296 | tf_op jit(solution)/shard_map/all_to_all | solution.py:105
  152.7 30.7 %collective-permute-start.16 = (bf16[2,64,1536]{2,1,0:T(8,128)(2,1)S(1)}, bf16[2,64,1536]{2,1,0:T(8,128)(2,1)S(1)}, u32[]{:S(2)}, u32[]{:S(2)}) collective-permute-start(bf16[2,64,1536]{2,1,0:T(8,128)(2,1)S(1)} %get-tuple-element.98.rest_0_), channel_id=1, source_target_pairs={{0,32},{1,33},{2,34},{3,35},{4,36},{5,37},{6,38},{7,39},{8,40},{9,... | collective-permute-start | bytes 1179656 | tf_op jit(solution)/shard_map/ppermute | solution.py:101
  155.4 28.0 %collective-permute-start.18 = (bf16[2,64,1536]{2,1,0:T(8,128)(2,1)S(1)}, bf16[2,64,1536]{2,1,0:T(8,128)(2,1)S(1)}, u32[]{:S(2)}, u32[]{:S(2)}) collective-permute-start(bf16[2,64,1536]{2,1,0:T(8,128)(2,1)S(1)} %get-tuple-element.100.rest_2_), channel_id=1, source_target_pairs={{0,96},{1,97},{2,98},{3,99},{4,100},{5,101},{6,102},{7,103},{8,104... | collective-permute-start | bytes 1179656 | tf_op jit(solution)/shard_map/ppermute | solution.py:101
  157.9 25.5 %collective-permute-start.17 = (bf16[2,64,1536]{2,1,0:T(8,128)(2,1)S(1)}, bf16[2,64,1536]{2,1,0:T(8,128)(2,1)}, u32[]{:S(2)}, u32[]{:S(2)}) collective-permute-start(bf16[2,64,1536]{2,1,0:T(8,128)(2,1)S(1)} %get-tuple-element.99.rest_1_), channel_id=1, source_target_pairs={{0,64},{1,65},{2,66},{3,67},{4,68},{5,69},{6,70},{7,71},{8,72},{9,... | collective-permute-start | bytes 1179656 | tf_op jit(solution)/shard_map/ppermute | solution.py:101
  163.1 6.6 %collective-permute-start.19 = (bf16[48,384]{1,0:T(8,128)(2,1)S(1)}, bf16[48,384]{1,0:T(8,128)(2,1)S(1)}, u32[]{:S(2)}, u32[]{:S(2)}) collective-permute-start(bf16[48,384]{1,0:T(8,128)(2,1)S(1)} %get-tuple-element.124), channel_id=1, source_target_pairs={{0,0},{1,16},{2,1},{3,17},{4,32},{5,48},{6,33},{7,49},{8,2},{9,18}... | collective-permute-start | bytes 110600 | tf_op jit(solution)/shard_map/ppermute | solution.py:101
  167.3 8.1 %collective-permute-start.20 = (bf16[48,384]{1,0:T(8,128)(2,1)S(1)}, bf16[48,384]{1,0:T(8,128)(2,1)S(1)}, u32[]{:S(2)}, u32[]{:S(2)}) collective-permute-start(bf16[48,384]{1,0:T(8,128)(2,1)S(1)} %get-tuple-element.125), channel_id=1, source_target_pairs={{0,1},{1,17},{2,0},{3,16},{4,33},{5,49},{6,32},{7,48},{8,3},{9,19}... | collective-permute-start | bytes 110600 | tf_op jit(solution)/shard_map/ppermute | solution.py:101
  169.7 9.1 %collective-permute-start.13 = (bf16[48,1152]{1,0:T(8,128)(2,1)S(1)}, bf16[48,1152]{1,0:T(8,128)(2,1)S(1)}, u32[]{:S(2)}, u32[]{:S(2)}) collective-permute-start(bf16[48,1152]{1,0:T(8,128)(2,1)S(1)} %get-tuple-element.112), channel_id=1, source_target_pairs={{0,64},{1,65},{2,66},{3,67},{4,68},{5,69},{6,70},{7,71},{8,72},{9,... | collective-permute-start | bytes 331784 | tf_op jit(solution)/shard_map/ppermute | solution.py:101
  180.2 5.7 %collective-permute-start.21 = (bf16[48,768]{1,0:T(8,128)(2,1)S(1)}, bf16[48,768]{1,0:T(8,128)(2,1)S(1)}, u32[]{:S(2)}, u32[]{:S(2)}) collective-permute-start(bf16[48,768]{1,0:T(8,128)(2,1)S(1)} %pad_maximum_fusion.13), channel_id=1, source_target_pairs={{0,64},{1,65},{2,66},{3,67},{4,68},{5,69},{6,70},{7,71},{8,72},{9,... | collective-permute-start | bytes 221192 | tf_op jit(solution)/shard_map/ppermute | solution.py:101
  186.0 8.0 %collective-permute-start.22 = (bf16[48,3072]{1,0:T(8,128)(2,1)S(1)}, bf16[48,3072]{1,0:T(8,128)(2,1)S(1)}, u32[]{:S(2)}, u32[]{:S(2)}) collective-permute-start(bf16[48,3072]{1,0:T(8,128)(2,1)S(1)} %fusion.20), channel_id=1, source_target_pairs={{0,32},{1,33},{2,34},{3,35},{4,36},{5,37},{6,38},{7,39},{8,40},{9,... | collective-permute-start | bytes 884744 | tf_op jit(solution)/shard_map/ppermute | solution.py:101
  (21 other events, 113.0 us)
where the time goes:
time: 199 us; the launch traced here: 197 us
  starting transfers between devices  59 us (30%)
  waiting for transfers between devices  53.6 us (27%)
  Pallas kernels  38.2 us (19%)
  local copies, waits for them, and re-layouts  24.3 us (12%)
  other arithmetic  16.7 us (8%)
  matrix products  2.61 us (1%)
  between operations  2.54 us (1%)
    ppermute x23, waiting for transfers between devices, send(): return lax.ppermute(array, AXES, pairs)  43.3 us
    ppermute x23, starting transfers between devices, send(): return lax.ppermute(array, AXES, pairs)  38.7 us
    all_to_all x4, starting transfers between devices, exchange(): lax.all_to_all(array, AXES, 0, 0, tiled=True, axis_index_groups=groups)  20.3 us
    all_to_all x4, waiting for transfers between devices, exchange(): lax.all_to_all(array, AXES, 0, 0, tiled=True, axis_index_groups=groups)  10.4 us
    pallas_call x1, Pallas kernels, terms(): pl.pallas_call(term_kernel, grid=(4,), in_specs=[pl.BlockSpec((depth, row...  7.94 us
    pallas_call x1, Pallas kernels, matmul_columns(): pl.pallas_call(functools.partial(product_kernel, ((1,), (0,)), False), gr...  6.97 us
    another operation x12, other arithmetic, in_order(): jnp.stack([jnp.where(bit == 0, mine, other), jnp.where(bit == 0, other, m...  6.73 us
    unnamed x36, local copies, waits for them, and re-layouts  6.35 us
  transfers between devices with their start and end apart: 27, of which 14 were waited for; matrix products, arithmetic and copies ran while one was open for 16% of the time, Pallas kernels for 8%

commit v1 on v0

--- a/solution.py
+++ b/solution.py
@@ -285,7 +285,7 @@
     for kind, out in enumerate((query_ref, key_ref, value_ref)):
         for step in range(2):
             at = step * wide + kind * HEAD_COLS
-            mine = mine_ref[:, at : at + HEAD_COLS]
+            mine = mine_ref[:, at : at + HEAD_COLS].astype(jnp.float32)
             theirs = theirs_ref[:, at : at + HEAD_COLS].astype(jnp.float32)
             low = jnp.where(core == 0, mine, theirs)
             high = jnp.where(core == 0, theirs, mine)
@@ -297,7 +297,7 @@
                     out[:, begin : begin + HEAD_COLS] = low
                     out[:, begin + HEAD_COLS : begin + 2 * HEAD_COLS] = high
 
-    mine = mine_ref[:, 2 * wide :]
+    mine = mine_ref[:, 2 * wide :].astype(jnp.float32)
     theirs = theirs_ref[:, 2 * wide :].astype(jnp.float32)
     output_ref[:, : 2 * HEAD_COLS] = jnp.where(core == 0, mine, theirs)
     output_ref[:, 2 * HEAD_COLS :] = jnp.where(core == 0, theirs, mine)
@@ -539,10 +539,11 @@
     before = send(other_qkv, Y_BEFORE).astype(jnp.float32)
     same = mine_qkv.astype(jnp.float32) + across
     cross = behind + before
-    sums = jnp.concatenate([same, cross], axis=1)
+    sums = jnp.concatenate([same.astype(jnp.bfloat16), cross.astype(jnp.bfloat16)], axis=1)
     across = after(send(mine_out, Y_ACROSS), sums).astype(jnp.float32)
-    mine = jnp.concatenate([sums, mine_out.astype(jnp.float32) + across], axis=1)
-    theirs = send(mine.astype(jnp.bfloat16), CORE_PARTNER)
+    total_out = (mine_out.astype(jnp.float32) + across).astype(jnp.bfloat16)
+    mine = jnp.concatenate([sums, total_out], axis=1)
+    theirs = send(mine, CORE_PARTNER)
     grad_query, grad_key, grad_value, grad_output = final_grads(core, y_lo, mine, theirs)
 
     a0, a1, a2, a3 = (after(part, sums) for part in arrived)

time: 199 us -> 198 us (level)
    unnamed x36 -> x38, local copies, waits for them, and re-layouts: 6.35 us -> 6.37 us
where the time goes in v1:
time: 198 us; the launch traced here: 197 us
  starting transfers between devices  59.7 us (30%)
  waiting for transfers between devices  53.9 us (27%)
  Pallas kernels  38.1 us (19%)
  local copies, waits for them, and re-layouts  24.3 us (12%)
  other arithmetic  15.7 us (8%)
  matrix products  2.61 us (1%)
  between operations  2.53 us (1%)
    ppermute x23, waiting for transfers between devices, send(): return lax.ppermute(array, AXES, pairs)  43.4 us
    ppermute x23, starting transfers between devices, send(): return lax.ppermute(array, AXES, pairs)  39.3 us
    all_to_all x4, starting transfers between devices, exchange(): lax.all_to_all(array, AXES, 0, 0, tiled=True, axis_index_groups=groups)  20.4 us
    all_to_all x4, waiting for transfers between devices, exchange(): lax.all_to_all(array, AXES, 0, 0, tiled=True, axis_index_groups=groups)  10.5 us
    pallas_call x1, Pallas kernels, terms(): pl.pallas_call(term_kernel, grid=(4,), in_specs=[pl.BlockSpec((depth, row...  7.94 us
    pallas_call x1, Pallas kernels, matmul_columns(): pl.pallas_call(functools.partial(product_kernel, ((1,), (0,)), False), gr...  6.98 us
    another operation x12, other arithmetic, in_order(): jnp.stack([jnp.where(bit == 0, mine, other), jnp.where(bit == 0, other, m...  6.7 us
    unnamed x38, local copies, waits for them, and re-layouts  6.37 us
  transfers between devices with their start and end apart: 27, of which 14 were waited for; matrix products, arithmetic and copies ran while one was open for 16% of the time, Pallas kernels for 8%

profile of v1, /device:TPU:3, one launch (start us, length us, event | category | flops | bytes accessed | tf_op | source)
XLA Modules:
  0.0 196.9 jit_solution(9438901815800309751)
XLA Ops:
  0.6 6.1 %collective-permute-start.2 = (bf16[48,1536]{1,0:T(8,128)(2,1)}, bf16[48,1536]{1,0:T(8,128)(2,1)S(1)}, u32[]{:S(2)}, u32[]{:S(2)}) collective-permute-start(bf16[48,1536]{1,0:T(8,128)(2,1)} %param.18), channel_id=1, source_target_pairs={{0,0},{16,1},{2,2},{18,3},{4,4},{20,5},{6,6},{22,7},{1,8},{17,9},{... | collective-permute-start | bytes 442376 | tf_op jit(solution)/shard_map/ppermute | solution.py:101
  13.6 2.6 %collective-permute-start.7 = (bf16[2,64,1536]{2,1,0:T(8,128)(2,1)}, bf16[2,64,1536]{2,1,0:T(8,128)(2,1)}, u32[]{:S(2)}, u32[]{:S(2)}) collective-permute-start(bf16[2,64,1536]{2,1,0:T(8,128)(2,1)} %get-tuple-element.91), channel_id=1, source_target_pairs={{0,64},{1,65},{2,66},{3,67},{4,68},{5,69},{6,70},{7,71},{8,72},{9,... | collective-permute-start | bytes 1179656 | tf_op jit(solution)/shard_map/ppermute | solution.py:101
  20.8 5.2 %all-to-all-start = ((bf16[4,2,48,2688]{3,2,1,0:T(8,128)(2,1)}), bf16[4,2,48,2688]{3,2,1,0:T(8,128)(2,1)S(1)}, u32[]{:S(2)}, u32[]{:S(2)}) async-start(bf16[4,2,48,2688]{3,2,1,0:T(8,128)(2,1)} %broadcast_in_dim.35), calls=%async_computation | async-start | bytes 4128768 | tf_op jit(solution)/shard_map/all_to_all | solution.py:105
  26.0 2.6 %copy.24 = bf16[512,1536]{0,1:T(8,128)(2,1)} copy(bf16[512,1536]{1,0:T(8,128)(2,1)} %param.14) | data formatting | bytes 3145728 | tf_op jit(solution)/shard_map/optimization_barrier | solution.py:117
  28.5 2.7 %copy.25 = bf16[512,4,4,96]{0,3,2,1:T(8,128)(2,1)} copy(bf16[512,4,4,96]{0,3,1,2:T(8,128)(2,1)} %bitcast.130) | data formatting | bytes 3145728 | tf_op jit(solution)/shard_map/transpose | solution.py:463
  33.8 2.7 %broadcast_select_fusion.weight_ref = bf16[512,1536]{1,0:T(8,128)(2,1)} fusion(bf16[512,1536]{1,0:T(8,128)(2,1)} %param.14, bf16[512,1536]{1,0:T(8,128)(2,1)} %copy.26, pred[]{:T(512)S(6)} %eq.32), kind=kLoop, calls=%fused_computation.11 | loop fusion | flops 786432 | bytes 4718593 | tf_op jit(solution)/shard_map/jit(_where)/select_n | solution.py:464
  50.1 5.0 %all-to-all-start.1 = ((bf16[4,384,1152]{2,1,0:T(8,128)(2,1)}), bf16[4,384,1152]{2,1,0:T(8,128)(2,1)}, u32[]{:S(2)}, u32[]{:S(2)}) async-start(bf16[4,384,1152]{2,1,0:T(8,128)(2,1)} %get-tuple-element.55), calls=%async_computation.1 | async-start | bytes 7077888 | tf_op jit(solution)/shard_map/all_to_all | solution.py:105
  59.3 3.8 %shard_map.155.a_ref.normed_ref = bf16[1024,1536]{1,0:T(8,128)(2,1)S(1)} custom-call(bf16[1024,512]{1,0:T(8,128)(2,1)S(1)} %bitcast.123, bf16[512,1536]{1,0:T(8,128)(2,1)S(1)} %copy-done.5), custom_call_target="tpu_custom_call" | custom-call | tf_op jit(solution)/shard_map/pallas_call | solution.py:127
  63.1 12.8 %collective-permute-done.9 = bf16[256,1536]{1,0:T(8,128)(2,1)} collective-permute-done((bf16[256,1536]{1,0:T(8,128)(2,1)S(1)}, bf16[256,1536]{1,0:T(8,128)(2,1)}, u32[]{:S(2)}, u32[]{:S(2)}) %collective-permute-start.9) | collective-permute-done | bytes 786464 | tf_op jit(solution)/shard_map/ppermute | solution.py:101
  82.6 7.0 %shard_map.157.qkv_ref = bf16[1024,1152]{1,0:T(8,128)(2,1)S(1)} custom-call(bf16[1024,1536]{1,0:T(8,128)(2,1)S(1)} %shard_map.155.a_ref.normed_ref, bf16[1536,1152]{1,0:T(8,128)(2,1)} %bitcast.24.b_ref), custom_call_target="tpu_custom_call" | custom-call | tf_op jit(solution)/shard_map/pallas_call | solution.py:182
  95.1 4.4 %shard_map.159 = (bf16[1024,384]{1,0:T(8,128)(2,1)S(1)}, bf16[1024,1152]{1,0:T(8,128)(2,1)S(1)}) custom-call(s32[8]{0:T(128)S(1)} %pad_add_fusion.limit_ref, bf16[1024,1152]{1,0:T(8,128)(2,1)S(1)} %shard_map.157.qkv_ref, bf16[1024,384]{1,0:T(8,128)(2,1)S(1)} %shard_map.158.d_att_ref), custom_call_target="tpu_custom_call" | custom-call | tf_op jit(solution)/shard_map/pallas_call | solution.py:370
  99.5 7.9 %shard_map.160 = bf16[4,384,1536]{2,1,0:T(8,128)(2,1)} custom-call(bf16[1024,1536]{1,0:T(8,128)(2,1)S(1)} %shard_map.155.a_ref.normed_ref, bf16[1024,1152]{1,0:T(8,128)(2,1)S(1)} %get-tuple-element.65.d_qkv_ref, bf16[1024,384]{1,0:T(8,128)(2,1)S(1)} %get-tuple-element.66.att_ref, bf16[1024,1536]{1,0:T(8,128)(2,1)S(1)} %bitcast.119), custom_call_target="tpu_custom_call" | custom-call | tf_op jit(solution)/shard_map/pallas_call | solution.py:243
  108.8 6.7 %all-to-all-start.2 = ((bf16[4,384,1536]{2,1,0:T(8,128)(2,1)}), bf16[4,384,1536]{2,1,0:T(8,128)(2,1)}, u32[]{:S(2)}, u32[]{:S(2)}) async-start(bf16[4,384,1536]{2,1,0:T(8,128)(2,1)} %shard_map.160), calls=%async_computation.2 | async-start | bytes 9437184 | tf_op jit(solution)/shard_map/all_to_all | solution.py:105
  121.2 16.7 %collective-permute-done.12 = bf16[256,1536]{1,0:T(8,128)(2,1)} collective-permute-done((bf16[256,1536]{1,0:T(8,128)(2,1)}, bf16[256,1536]{1,0:T(8,128)(2,1)}, u32[]{:S(2)}, u32[]{:S(2)}) %collective-permute-start.12) | collective-permute-done | bytes 786464 | tf_op jit(solution)/shard_map/ppermute | solution.py:101
  140.3 3.9 %all-to-all-done.2.parts_ref = bf16[4,384,1536]{2,1,0:T(8,128)(2,1)} async-done(((bf16[4,384,1536]{2,1,0:T(8,128)(2,1)}), bf16[4,384,1536]{2,1,0:T(8,128)(2,1)}, u32[]{:S(2)}, u32[]{:S(2)}) %all-to-all-start.2) | async-done | bytes 4718624 | tf_op jit(solution)/shard_map/all_to_all | solution.py:105
  144.1 4.3 %shard_map.163 = bf16[384,1536]{1,0:T(8,128)(2,1)} custom-call(bf16[4,384,1536]{2,1,0:T(8,128)(2,1)} %all-to-all-done.2.parts_ref, bf16[2,64,1536]{2,1,0:T(8,128)(2,1)S(1)} %get-tuple-element.98.rest_0_, bf16[2,64,1536]{2,1,0:T(8,128)(2,1)S(1)} %get-tuple-element.99.rest_1_, bf16[2,64,1536]{2,1,0:T(8,128)(2,1)S(1)} %get-tuple-element.100.rest_2_), custom_call_target="tpu_custom_call" | custom-call | tf_op jit(solution)/shard_map/pallas_call | solution.py:271
  148.5 3.6 %all-to-all-start.3 = ((bf16[4,96,1536]{2,1,0:T(8,128)(2,1)}), bf16[4,96,1536]{2,1,0:T(8,128)(2,1)S(1)}, u32[]{:S(2)}, u32[]{:S(2)}) async-start(bf16[4,96,1536]{2,1,0:T(8,128)(2,1)} %bitcast.49), calls=%async_computation.3 | async-start | bytes 2359296 | tf_op jit(solution)/shard_map/all_to_all | solution.py:105
  152.7 2.6 %collective-permute-start.16 = (bf16[2,64,1536]{2,1,0:T(8,128)(2,1)S(1)}, bf16[2,64,1536]{2,1,0:T(8,128)(2,1)S(1)}, u32[]{:S(2)}, u32[]{:S(2)}) collective-permute-start(bf16[2,64,1536]{2,1,0:T(8,128)(2,1)S(1)} %get-tuple-element.98.rest_0_), channel_id=1, source_target_pairs={{0,32},{1,33},{2,34},{3,35},{4,36},{5,37},{6,38},{7,39},{8,40},{9,... | collective-permute-start | bytes 1179656 | tf_op jit(solution)/shard_map/ppermute | solution.py:101
  155.3 2.6 %collective-permute-start.18 = (bf16[2,64,1536]{2,1,0:T(8,128)(2,1)S(1)}, bf16[2,64,1536]{2,1,0:T(8,128)(2,1)S(1)}, u32[]{:S(2)}, u32[]{:S(2)}) collective-permute-start(bf16[2,64,1536]{2,1,0:T(8,128)(2,1)S(1)} %get-tuple-element.100.rest_2_), channel_id=1, source_target_pairs={{0,96},{1,97},{2,98},{3,99},{4,100},{5,101},{6,102},{7,103},{8,104... | collective-permute-start | bytes 1179656 | tf_op jit(solution)/shard_map/ppermute | solution.py:101
  158.1 4.7 %all-to-all-done.3.parts_ref = bf16[4,96,1536]{2,1,0:T(8,128)(2,1)S(1)} async-done(((bf16[4,96,1536]{2,1,0:T(8,128)(2,1)}), bf16[4,96,1536]{2,1,0:T(8,128)(2,1)S(1)}, u32[]{:S(2)}, u32[]{:S(2)}) %all-to-all-start.3) | async-done | bytes 1179680 | tf_op jit(solution)/shard_map/all_to_all | solution.py:105
  163.1 4.1 %collective-permute-start.19 = (bf16[48,384]{1,0:T(8,128)(2,1)S(1)}, bf16[48,384]{1,0:T(8,128)(2,1)S(1)}, u32[]{:S(2)}, u32[]{:S(2)}) collective-permute-start(bf16[48,384]{1,0:T(8,128)(2,1)S(1)} %get-tuple-element.124), channel_id=1, source_target_pairs={{0,0},{1,16},{2,1},{3,17},{4,32},{5,48},{6,33},{7,49},{8,2},{9,18}... | collective-permute-start | bytes 110600 | tf_op jit(solution)/shard_map/ppermute | solution.py:101
  171.4 4.0 %collective-permute-done.20 = bf16[48,384]{1,0:T(8,128)(2,1)S(1)} collective-permute-done((bf16[48,384]{1,0:T(8,128)(2,1)S(1)}, bf16[48,384]{1,0:T(8,128)(2,1)S(1)}, u32[]{:S(2)}, u32[]{:S(2)}) %collective-permute-start.20) | collective-permute-done | bytes 36896 | tf_op jit(solution)/shard_map/ppermute | solution.py:101
  175.4 3.3 %collective-permute-done.13 = bf16[48,1152]{1,0:T(8,128)(2,1)S(1)} collective-permute-done((bf16[48,1152]{1,0:T(8,128)(2,1)S(1)}, bf16[48,1152]{1,0:T(8,128)(2,1)S(1)}, u32[]{:S(2)}, u32[]{:S(2)}) %collective-permute-start.13) | collective-permute-done | bytes 110624 | tf_op jit(solution)/shard_map/ppermute | solution.py:101
  185.1 7.5 %collective-permute-start.22 = (bf16[48,3072]{1,0:T(8,128)(2,1)S(1)}, bf16[48,3072]{1,0:T(8,128)(2,1)S(1)}, u32[]{:S(2)}, u32[]{:S(2)}) collective-permute-start(bf16[48,3072]{1,0:T(8,128)(2,1)S(1)} %pad_maximum_fusion.8.mine_ref), channel_id=1, source_target_pairs={{0,32},{1,33},{2,34},{3,35},{4,36},{5,37},{6,38},{7,39},{8,40},{9,... | collective-permute-start | bytes 884744 | tf_op jit(solution)/shard_map/ppermute | solution.py:101
  (150 shorter events, 67.8 us)
Async XLA Ops:
  0.6 18.6 %collective-permute-start.2 = (bf16[48,1536]{1,0:T(8,128)(2,1)}, bf16[48,1536]{1,0:T(8,128)(2,1)S(1)}, u32[]{:S(2)}, u32[]{:S(2)}) collective-permute-start(bf16[48,1536]{1,0:T(8,128)(2,1)} %param.18), channel_id=1, source_target_pairs={{0,0},{16,1},{2,2},{18,3},{4,4},{20,5},{6,6},{22,7},{1,8},{17,9},{... | collective-permute-start | bytes 442376 | tf_op jit(solution)/shard_map/ppermute | solution.py:101
  6.7 12.5 %collective-permute-start.3 = (bf16[48,1536]{1,0:T(8,128)(2,1)}, bf16[48,1536]{1,0:T(8,128)(2,1)S(1)}, u32[]{:S(2)}, u32[]{:S(2)}) collective-permute-start(bf16[48,1536]{1,0:T(8,128)(2,1)} %param.18), channel_id=1, source_target_pairs={{1,0},{17,1},{3,2},{19,3},{5,4},{21,5},{7,6},{23,7},{0,8},{16,9},{... | collective-permute-start | bytes 442376 | tf_op jit(solution)/shard_map/ppermute | solution.py:101
  10.3 6.9 %collective-permute-start = (bf16[48,1152]{1,0:T(8,128)(2,1)S(1)}, bf16[48,1152]{1,0:T(8,128)(2,1)S(1)}, u32[]{:S(2)}, u32[]{:S(2)}) collective-permute-start(bf16[48,1152]{1,0:T(8,128)(2,1)S(1)} %pad_maximum_fusion.12), channel_id=1, source_target_pairs={{0,1},{1,0},{2,3},{3,2},{4,5},{5,4},{6,7},{7,6},{8,9},{9,8},{10,11... | collective-permute-start | bytes 331784 | tf_op jit(solution)/shard_map/ppermute | solution.py:101
  13.6 41.5 %collective-permute-start.7 = (bf16[2,64,1536]{2,1,0:T(8,128)(2,1)}, bf16[2,64,1536]{2,1,0:T(8,128)(2,1)}, u32[]{:S(2)}, u32[]{:S(2)}) collective-permute-start(bf16[2,64,1536]{2,1,0:T(8,128)(2,1)} %get-tuple-element.91), channel_id=1, source_target_pairs={{0,64},{1,65},{2,66},{3,67},{4,68},{5,69},{6,70},{7,71},{8,72},{9,... | collective-permute-start | bytes 1179656 | tf_op jit(solution)/shard_map/ppermute | solution.py:101
  16.3 38.9 %collective-permute-start.8 = (bf16[2,64,1536]{2,1,0:T(8,128)(2,1)}, bf16[2,64,1536]{2,1,0:T(8,128)(2,1)}, u32[]{:S(2)}, u32[]{:S(2)}) collective-permute-start(bf16[2,64,1536]{2,1,0:T(8,128)(2,1)} %get-tuple-element.90), channel_id=1, source_target_pairs={{0,96},{1,97},{2,98},{3,99},{4,100},{5,101},{6,102},{7,103},{8,104... | collective-permute-start | bytes 1179656 | tf_op jit(solution)/shard_map/ppermute | solution.py:101
  17.3 21.0 %collective-permute-start.1 = (bf16[2,2,64,512]{3,2,1,0:T(8,128)(2,1)S(1)}, bf16[2,2,64,512]{3,2,1,0:T(8,128)(2,1)S(1)}, u32[]{:S(2)}, u32[]{:S(2)}) collective-permute-start(bf16[2,2,64,512]{3,2,1,0:T(8,128)(2,1)S(1)} %bitcast.135), channel_id=1, source_target_pairs={{0,1},{1,2},{2,3},{3,4},{4,5},{5,6},{6,7},{7,8},{8,9},{9,10},{10,1... | collective-permute-start | bytes 786440 | tf_op jit(solution)/shard_map/ppermute | solution.py:101
  20.8 25.8 %all-to-all-start = ((bf16[4,2,48,2688]{3,2,1,0:T(8,128)(2,1)}), bf16[4,2,48,2688]{3,2,1,0:T(8,128)(2,1)S(1)}, u32[]{:S(2)}, u32[]{:S(2)}) async-start(bf16[4,2,48,2688]{3,2,1,0:T(8,128)(2,1)} %broadcast_in_dim.35), calls=%async_computation | async-start | bytes 4128768 | tf_op jit(solution)/shard_map/all_to_all | solution.py:105
  36.6 18.6 %collective-permute-start.6 = (bf16[2,64,1536]{2,1,0:T(8,128)(2,1)}, bf16[2,64,1536]{2,1,0:T(8,128)(2,1)}, u32[]{:S(2)}, u32[]{:S(2)}) collective-permute-start(bf16[2,64,1536]{2,1,0:T(8,128)(2,1)} %get-tuple-element.58), channel_id=1, source_target_pairs={{0,32},{1,33},{2,34},{3,35},{4,36},{5,37},{6,38},{7,39},{8,40},{9,... | collective-permute-start | bytes 1179656 | tf_op jit(solution)/shard_map/ppermute | solution.py:101
  41.6 13.6 %collective-permute-start.4 = (bf16[256,512]{1,0:T(8,128)(2,1)S(1)}, bf16[256,512]{1,0:T(8,128)(2,1)S(1)}, u32[]{:S(2)}, u32[]{:S(2)}) collective-permute-start(bf16[256,512]{1,0:T(8,128)(2,1)S(1)} %fusion.3), channel_id=1, source_target_pairs={{0,1},{1,0},{2,3},{3,2},{4,5},{5,4},{6,7},{7,6},{8,9},{9,8},{10,11... | collective-permute-start | bytes 786440 | tf_op jit(solution)/shard_map/ppermute | solution.py:101
  50.1 27.8 %all-to-all-start.1 = ((bf16[4,384,1152]{2,1,0:T(8,128)(2,1)}), bf16[4,384,1152]{2,1,0:T(8,128)(2,1)}, u32[]{:S(2)}, u32[]{:S(2)}) async-start(bf16[4,384,1152]{2,1,0:T(8,128)(2,1)} %get-tuple-element.55), calls=%async_computation.1 | async-start | bytes 7077888 | tf_op jit(solution)/shard_map/all_to_all | solution.py:105
  57.1 18.8 %collective-permute-start.9 = (bf16[256,1536]{1,0:T(8,128)(2,1)S(1)}, bf16[256,1536]{1,0:T(8,128)(2,1)}, u32[]{:S(2)}, u32[]{:S(2)}) collective-permute-start(bf16[256,1536]{1,0:T(8,128)(2,1)S(1)} %bitcast_select_fusion), channel_id=1, source_target_pairs={{0,1},{1,0},{2,3},{3,2},{4,5},{5,4},{6,7},{7,6},{8,9},{9,8},{10,11... | collective-permute-start | bytes 2359304 | tf_op jit(solution)/shard_map/ppermute | solution.py:101
  81.1 8.5 %collective-permute-start.10 = (bf16[2,256,1536]{2,1,0:T(8,128)(2,1)}, bf16[2,256,1536]{2,1,0:T(8,128)(2,1)}, u32[]{:S(2)}, u32[]{:S(2)}) collective-permute-start(bf16[2,256,1536]{2,1,0:T(8,128)(2,1)} %pad_maximum_fusion.1), channel_id=1, source_target_pairs={{0,32},{1,33},{2,34},{3,35},{4,36},{5,37},{6,38},{7,39},{8,40},{9,... | collective-permute-start | bytes 4718600 | tf_op jit(solution)/shard_map/ppermute | solution.py:101
  108.7 6.8 %collective-permute-start.11 = (bf16[512,1536]{1,0:T(8,128)(2,1)S(1)}, bf16[512,1536]{1,0:T(8,128)(2,1)}, u32[]{:S(2)}, u32[]{:S(2)}) collective-permute-start(bf16[512,1536]{1,0:T(8,128)(2,1)S(1)} %shard_map.161), channel_id=1, source_target_pairs={{0,32},{1,33},{2,34},{3,35},{4,36},{5,37},{6,38},{7,39},{8,40},{9,... | collective-permute-start | bytes 4718600 | tf_op jit(solution)/shard_map/ppermute | solution.py:101
  108.8 35.3 %all-to-all-start.2 = ((bf16[4,384,1536]{2,1,0:T(8,128)(2,1)}), bf16[4,384,1536]{2,1,0:T(8,128)(2,1)}, u32[]{:S(2)}, u32[]{:S(2)}) async-start(bf16[4,384,1536]{2,1,0:T(8,128)(2,1)} %shard_map.160), calls=%async_computation.2 | async-start | bytes 9437184 | tf_op jit(solution)/shard_map/all_to_all | solution.py:105
  118.8 19.2 %collective-permute-start.12 = (bf16[256,1536]{1,0:T(8,128)(2,1)}, bf16[256,1536]{1,0:T(8,128)(2,1)}, u32[]{:S(2)}, u32[]{:S(2)}) collective-permute-start(bf16[256,1536]{1,0:T(8,128)(2,1)} %dynamic-slice_bitcast_fusion), channel_id=1, source_target_pairs={{0,1},{1,0},{2,3},{3,2},{4,5},{5,4},{6,7},{7,6},{8,9},{9,8},{10,11... | collective-permute-start | bytes 2359304 | tf_op jit(solution)/shard_map/ppermute | solution.py:101
  148.5 14.3 %all-to-all-start.3 = ((bf16[4,96,1536]{2,1,0:T(8,128)(2,1)}), bf16[4,96,1536]{2,1,0:T(8,128)(2,1)S(1)}, u32[]{:S(2)}, u32[]{:S(2)}) async-start(bf16[4,96,1536]{2,1,0:T(8,128)(2,1)} %bitcast.49), calls=%async_computation.3 | async-start | bytes 2359296 | tf_op jit(solution)/shard_map/all_to_all | solution.py:105
  152.7 30.7 %collective-permute-start.16 = (bf16[2,64,1536]{2,1,0:T(8,128)(2,1)S(1)}, bf16[2,64,1536]{2,1,0:T(8,128)(2,1)S(1)}, u32[]{:S(2)}, u32[]{:S(2)}) collective-permute-start(bf16[2,64,1536]{2,1,0:T(8,128)(2,1)S(1)} %get-tuple-element.98.rest_0_), channel_id=1, source_target_pairs={{0,32},{1,33},{2,34},{3,35},{4,36},{5,37},{6,38},{7,39},{8,40},{9,... | collective-permute-start | bytes 1179656 | tf_op jit(solution)/shard_map/ppermute | solution.py:101
  155.3 28.1 %collective-permute-start.18 = (bf16[2,64,1536]{2,1,0:T(8,128)(2,1)S(1)}, bf16[2,64,1536]{2,1,0:T(8,128)(2,1)S(1)}, u32[]{:S(2)}, u32[]{:S(2)}) collective-permute-start(bf16[2,64,1536]{2,1,0:T(8,128)(2,1)S(1)} %get-tuple-element.100.rest_2_), channel_id=1, source_target_pairs={{0,96},{1,97},{2,98},{3,99},{4,100},{5,101},{6,102},{7,103},{8,104... | collective-permute-start | bytes 1179656 | tf_op jit(solution)/shard_map/ppermute | solution.py:101
  157.9 25.5 %collective-permute-start.17 = (bf16[2,64,1536]{2,1,0:T(8,128)(2,1)S(1)}, bf16[2,64,1536]{2,1,0:T(8,128)(2,1)}, u32[]{:S(2)}, u32[]{:S(2)}) collective-permute-start(bf16[2,64,1536]{2,1,0:T(8,128)(2,1)S(1)} %get-tuple-element.99.rest_1_), channel_id=1, source_target_pairs={{0,64},{1,65},{2,66},{3,67},{4,68},{5,69},{6,70},{7,71},{8,72},{9,... | collective-permute-start | bytes 1179656 | tf_op jit(solution)/shard_map/ppermute | solution.py:101
  163.1 6.6 %collective-permute-start.19 = (bf16[48,384]{1,0:T(8,128)(2,1)S(1)}, bf16[48,384]{1,0:T(8,128)(2,1)S(1)}, u32[]{:S(2)}, u32[]{:S(2)}) collective-permute-start(bf16[48,384]{1,0:T(8,128)(2,1)S(1)} %get-tuple-element.124), channel_id=1, source_target_pairs={{0,0},{1,16},{2,1},{3,17},{4,32},{5,48},{6,33},{7,49},{8,2},{9,18}... | collective-permute-start | bytes 110600 | tf_op jit(solution)/shard_map/ppermute | solution.py:101
  167.2 8.1 %collective-permute-start.20 = (bf16[48,384]{1,0:T(8,128)(2,1)S(1)}, bf16[48,384]{1,0:T(8,128)(2,1)S(1)}, u32[]{:S(2)}, u32[]{:S(2)}) collective-permute-start(bf16[48,384]{1,0:T(8,128)(2,1)S(1)} %get-tuple-element.125), channel_id=1, source_target_pairs={{0,1},{1,17},{2,0},{3,16},{4,33},{5,49},{6,32},{7,48},{8,3},{9,19}... | collective-permute-start | bytes 110600 | tf_op jit(solution)/shard_map/ppermute | solution.py:101
  169.7 9.0 %collective-permute-start.13 = (bf16[48,1152]{1,0:T(8,128)(2,1)S(1)}, bf16[48,1152]{1,0:T(8,128)(2,1)S(1)}, u32[]{:S(2)}, u32[]{:S(2)}) collective-permute-start(bf16[48,1152]{1,0:T(8,128)(2,1)S(1)} %get-tuple-element.112), channel_id=1, source_target_pairs={{0,64},{1,65},{2,66},{3,67},{4,68},{5,69},{6,70},{7,71},{8,72},{9,... | collective-permute-start | bytes 331784 | tf_op jit(solution)/shard_map/ppermute | solution.py:101
  180.2 4.8 %collective-permute-start.21 = (bf16[48,768]{1,0:T(8,128)(2,1)S(1)}, bf16[48,768]{1,0:T(8,128)(2,1)S(1)}, u32[]{:S(2)}, u32[]{:S(2)}) collective-permute-start(bf16[48,768]{1,0:T(8,128)(2,1)S(1)} %pad_maximum_fusion.13), channel_id=1, source_target_pairs={{0,64},{1,65},{2,66},{3,67},{4,68},{5,69},{6,70},{7,71},{8,72},{9,... | collective-permute-start | bytes 221192 | tf_op jit(solution)/shard_map/ppermute | solution.py:101
  185.1 8.9 %collective-permute-start.22 = (bf16[48,3072]{1,0:T(8,128)(2,1)S(1)}, bf16[48,3072]{1,0:T(8,128)(2,1)S(1)}, u32[]{:S(2)}, u32[]{:S(2)}) collective-permute-start(bf16[48,3072]{1,0:T(8,128)(2,1)S(1)} %pad_maximum_fusion.8.mine_ref), channel_id=1, source_target_pairs={{0,32},{1,33},{2,34},{3,35},{4,36},{5,37},{6,38},{7,39},{8,40},{9,... | collective-permute-start | bytes 884744 | tf_op jit(solution)/shard_map/ppermute | solution.py:101
  (22 other events, 112.6 us)

commit v2 on v1

--- a/solution.py
+++ b/solution.py
@@ -213,7 +213,7 @@
         ],
         out_shape=[
             pltpu.HBM((4, rows, 3 * HEAD_COLS), jnp.bfloat16),
-            jax.ShapeDtypeStruct((rows, width), jnp.bfloat16),
+            pltpu.HBM((rows, width), jnp.bfloat16),
         ],
         compiler_params=pltpu.CompilerParams(vmem_limit_bytes=32 * 1024 * 1024),
         cost_estimate=NO_COST,

time: 198 us -> 198 us (level)
    unnamed x38 -> x36, local copies, waits for them, and re-layouts: 6.37 us -> 5.31 us
where the time goes in v2:
time: 198 us; the launch traced here: 196 us
  starting transfers between devices  59.7 us (30%)
  waiting for transfers between devices  53.8 us (27%)
  Pallas kernels  38.6 us (19%)
  local copies, waits for them, and re-layouts  23.3 us (12%)
  other arithmetic  15.8 us (8%)
  matrix products  2.61 us (1%)
  between operations  2.55 us (1%)
    ppermute x23, waiting for transfers between devices, send(): return lax.ppermute(array, AXES, pairs)  43.4 us
    ppermute x23, starting transfers between devices, send(): return lax.ppermute(array, AXES, pairs)  39.4 us
    all_to_all x4, starting transfers between devices, exchange(): lax.all_to_all(array, AXES, 0, 0, tiled=True, axis_index_groups=groups)  20.3 us
    all_to_all x4, waiting for transfers between devices, exchange(): lax.all_to_all(array, AXES, 0, 0, tiled=True, axis_index_groups=groups)  10.4 us
    pallas_call x1, Pallas kernels, terms(): pl.pallas_call(term_kernel, grid=(4,), in_specs=[pl.BlockSpec((depth, row...  7.94 us
    pallas_call x1, Pallas kernels, matmul_columns(): pl.pallas_call(functools.partial(product_kernel, ((1,), (0,)), False), gr...  6.97 us
    another operation x12, other arithmetic, in_order(): jnp.stack([jnp.where(bit == 0, mine, other), jnp.where(bit == 0, other, m...  6.73 us
    pallas_call x3, Pallas kernels, matmul(): pl.pallas_call(functools.partial(product_kernel, ((dims[0],), (dims[1],))...  5.85 us
  transfers between devices with their start and end apart: 27, of which 14 were waited for; matrix products, arithmetic and copies ran while one was open for 16% of the time, Pallas kernels for 8%

profile of v2, /device:TPU:3, one launch (start us, length us, event | category | flops | bytes accessed | tf_op | source)
XLA Modules:
  0.0 196.3 jit_solution(2136040672871201771)
XLA Ops:
  0.6 6.1 %collective-permute-start.2 = (bf16[48,1536]{1,0:T(8,128)(2,1)}, bf16[48,1536]{1,0:T(8,128)(2,1)S(1)}, u32[]{:S(2)}, u32[]{:S(2)}) collective-permute-start(bf16[48,1536]{1,0:T(8,128)(2,1)} %param.18), channel_id=1, source_target_pairs={{0,0},{16,1},{2,2},{18,3},{4,4},{20,5},{6,6},{22,7},{1,8},{17,9},{... | collective-permute-start | bytes 442376 | tf_op jit(solution)/shard_map/ppermute | solution.py:101
  13.6 2.6 %collective-permute-start.7 = (bf16[2,64,1536]{2,1,0:T(8,128)(2,1)}, bf16[2,64,1536]{2,1,0:T(8,128)(2,1)}, u32[]{:S(2)}, u32[]{:S(2)}) collective-permute-start(bf16[2,64,1536]{2,1,0:T(8,128)(2,1)} %get-tuple-element.91), channel_id=1, source_target_pairs={{0,64},{1,65},{2,66},{3,67},{4,68},{5,69},{6,70},{7,71},{8,72},{9,... | collective-permute-start | bytes 1179656 | tf_op jit(solution)/shard_map/ppermute | solution.py:101
  20.8 5.2 %all-to-all-start = ((bf16[4,2,48,2688]{3,2,1,0:T(8,128)(2,1)}), bf16[4,2,48,2688]{3,2,1,0:T(8,128)(2,1)S(1)}, u32[]{:S(2)}, u32[]{:S(2)}) async-start(bf16[4,2,48,2688]{3,2,1,0:T(8,128)(2,1)} %broadcast_in_dim.35), calls=%async_computation | async-start | bytes 4128768 | tf_op jit(solution)/shard_map/all_to_all | solution.py:105
  26.0 2.6 %copy.24 = bf16[512,1536]{0,1:T(8,128)(2,1)} copy(bf16[512,1536]{1,0:T(8,128)(2,1)} %param.14) | data formatting | bytes 3145728 | tf_op jit(solution)/shard_map/optimization_barrier | solution.py:117
  28.5 2.7 %copy.25 = bf16[512,4,4,96]{0,3,2,1:T(8,128)(2,1)} copy(bf16[512,4,4,96]{0,3,1,2:T(8,128)(2,1)} %bitcast.130) | data formatting | bytes 3145728 | tf_op jit(solution)/shard_map/transpose | solution.py:463
  33.8 2.7 %broadcast_select_fusion.weight_ref = bf16[512,1536]{1,0:T(8,128)(2,1)} fusion(bf16[512,1536]{1,0:T(8,128)(2,1)} %param.14, bf16[512,1536]{1,0:T(8,128)(2,1)} %copy.26, pred[]{:T(512)S(6)} %eq.32), kind=kLoop, calls=%fused_computation.11 | loop fusion | flops 786432 | bytes 4718593 | tf_op jit(solution)/shard_map/jit(_where)/select_n | solution.py:464
  46.6 2.8 %shard_map.156 = (bf16[4,384,1152]{2,1,0:T(8,128)(2,1)}, bf16[384,1536]{1,0:T(8,128)(2,1)}) custom-call(bf16[384,2688]{1,0:T(8,128)(2,1)S(1)} %bitcast.120), custom_call_target="tpu_custom_call" | custom-call | tf_op jit(solution)/shard_map/pallas_call | solution.py:206
  49.4 5.0 %all-to-all-start.1 = ((bf16[4,384,1152]{2,1,0:T(8,128)(2,1)}), bf16[4,384,1152]{2,1,0:T(8,128)(2,1)}, u32[]{:S(2)}, u32[]{:S(2)}) async-start(bf16[4,384,1152]{2,1,0:T(8,128)(2,1)} %get-tuple-element.55), calls=%async_computation.1 | async-start | bytes 7077888 | tf_op jit(solution)/shard_map/all_to_all | solution.py:105
  58.7 3.8 %shard_map.155.a_ref.normed_ref = bf16[1024,1536]{1,0:T(8,128)(2,1)S(1)} custom-call(bf16[1024,512]{1,0:T(8,128)(2,1)S(1)} %bitcast.123, bf16[512,1536]{1,0:T(8,128)(2,1)S(1)} %copy-done.4), custom_call_target="tpu_custom_call" | custom-call | tf_op jit(solution)/shard_map/pallas_call | solution.py:127
  62.5 12.8 %collective-permute-done.9 = bf16[256,1536]{1,0:T(8,128)(2,1)} collective-permute-done((bf16[256,1536]{1,0:T(8,128)(2,1)S(1)}, bf16[256,1536]{1,0:T(8,128)(2,1)}, u32[]{:S(2)}, u32[]{:S(2)}) %collective-permute-start.9) | collective-permute-done | bytes 786464 | tf_op jit(solution)/shard_map/ppermute | solution.py:101
  82.0 7.0 %shard_map.157.qkv_ref = bf16[1024,1152]{1,0:T(8,128)(2,1)S(1)} custom-call(bf16[1024,1536]{1,0:T(8,128)(2,1)S(1)} %shard_map.155.a_ref.normed_ref, bf16[1536,1152]{1,0:T(8,128)(2,1)} %bitcast.24.b_ref), custom_call_target="tpu_custom_call" | custom-call | tf_op jit(solution)/shard_map/pallas_call | solution.py:182
  94.5 4.4 %shard_map.159 = (bf16[1024,384]{1,0:T(8,128)(2,1)S(1)}, bf16[1024,1152]{1,0:T(8,128)(2,1)S(1)}) custom-call(s32[8]{0:T(128)S(1)} %pad_add_fusion.limit_ref, bf16[1024,1152]{1,0:T(8,128)(2,1)S(1)} %shard_map.157.qkv_ref, bf16[1024,384]{1,0:T(8,128)(2,1)S(1)} %shard_map.158.d_att_ref), custom_call_target="tpu_custom_call" | custom-call | tf_op jit(solution)/shard_map/pallas_call | solution.py:370
  98.9 7.9 %shard_map.160 = bf16[4,384,1536]{2,1,0:T(8,128)(2,1)} custom-call(bf16[1024,1536]{1,0:T(8,128)(2,1)S(1)} %shard_map.155.a_ref.normed_ref, bf16[1024,1152]{1,0:T(8,128)(2,1)S(1)} %get-tuple-element.65.d_qkv_ref, bf16[1024,384]{1,0:T(8,128)(2,1)S(1)} %get-tuple-element.66.att_ref, bf16[1024,1536]{1,0:T(8,128)(2,1)S(1)} %bitcast.119), custom_call_target="tpu_custom_call" | custom-call | tf_op jit(solution)/shard_map/pallas_call | solution.py:243
  108.2 6.7 %all-to-all-start.2 = ((bf16[4,384,1536]{2,1,0:T(8,128)(2,1)}), bf16[4,384,1536]{2,1,0:T(8,128)(2,1)}, u32[]{:S(2)}, u32[]{:S(2)}) async-start(bf16[4,384,1536]{2,1,0:T(8,128)(2,1)} %shard_map.160), calls=%async_computation.2 | async-start | bytes 9437184 | tf_op jit(solution)/shard_map/all_to_all | solution.py:105
  120.6 16.7 %collective-permute-done.12 = bf16[256,1536]{1,0:T(8,128)(2,1)} collective-permute-done((bf16[256,1536]{1,0:T(8,128)(2,1)}, bf16[256,1536]{1,0:T(8,128)(2,1)}, u32[]{:S(2)}, u32[]{:S(2)}) %collective-permute-start.12) | collective-permute-done | bytes 786464 | tf_op jit(solution)/shard_map/ppermute | solution.py:101
  139.7 3.9 %all-to-all-done.2.parts_ref = bf16[4,384,1536]{2,1,0:T(8,128)(2,1)} async-done(((bf16[4,384,1536]{2,1,0:T(8,128)(2,1)}), bf16[4,384,1536]{2,1,0:T(8,128)(2,1)}, u32[]{:S(2)}, u32[]{:S(2)}) %all-to-all-start.2) | async-done | bytes 4718624 | tf_op jit(solution)/shard_map/all_to_all | solution.py:105
  143.5 4.3 %shard_map.163 = bf16[384,1536]{1,0:T(8,128)(2,1)} custom-call(bf16[4,384,1536]{2,1,0:T(8,128)(2,1)} %all-to-all-done.2.parts_ref, bf16[2,64,1536]{2,1,0:T(8,128)(2,1)S(1)} %get-tuple-element.98.rest_0_, bf16[2,64,1536]{2,1,0:T(8,128)(2,1)S(1)} %get-tuple-element.99.rest_1_, bf16[2,64,1536]{2,1,0:T(8,128)(2,1)S(1)} %get-tuple-element.100.rest_2_), custom_call_target="tpu_custom_call" | custom-call | tf_op jit(solution)/shard_map/pallas_call | solution.py:271
  147.9 3.6 %all-to-all-start.3 = ((bf16[4,96,1536]{2,1,0:T(8,128)(2,1)}), bf16[4,96,1536]{2,1,0:T(8,128)(2,1)S(1)}, u32[]{:S(2)}, u32[]{:S(2)}) async-start(bf16[4,96,1536]{2,1,0:T(8,128)(2,1)} %bitcast.49), calls=%async_computation.3 | async-start | bytes 2359296 | tf_op jit(solution)/shard_map/all_to_all | solution.py:105
  152.1 2.6 %collective-permute-start.16 = (bf16[2,64,1536]{2,1,0:T(8,128)(2,1)S(1)}, bf16[2,64,1536]{2,1,0:T(8,128)(2,1)S(1)}, u32[]{:S(2)}, u32[]{:S(2)}) collective-permute-start(bf16[2,64,1536]{2,1,0:T(8,128)(2,1)S(1)} %get-tuple-element.98.rest_0_), channel_id=1, source_target_pairs={{0,32},{1,33},{2,34},{3,35},{4,36},{5,37},{6,38},{7,39},{8,40},{9,... | collective-permute-start | bytes 1179656 | tf_op jit(solution)/shard_map/ppermute | solution.py:101
  157.6 4.6 %all-to-all-done.3.parts_ref = bf16[4,96,1536]{2,1,0:T(8,128)(2,1)S(1)} async-done(((bf16[4,96,1536]{2,1,0:T(8,128)(2,1)}), bf16[4,96,1536]{2,1,0:T(8,128)(2,1)S(1)}, u32[]{:S(2)}, u32[]{:S(2)}) %all-to-all-start.3) | async-done | bytes 1179680 | tf_op jit(solution)/shard_map/all_to_all | solution.py:105
  162.5 4.1 %collective-permute-start.19 = (bf16[48,384]{1,0:T(8,128)(2,1)S(1)}, bf16[48,384]{1,0:T(8,128)(2,1)S(1)}, u32[]{:S(2)}, u32[]{:S(2)}) collective-permute-start(bf16[48,384]{1,0:T(8,128)(2,1)S(1)} %get-tuple-element.124), channel_id=1, source_target_pairs={{0,0},{1,16},{2,1},{3,17},{4,32},{5,48},{6,33},{7,49},{8,2},{9,18}... | collective-permute-start | bytes 110600 | tf_op jit(solution)/shard_map/ppermute | solution.py:101
  170.8 4.0 %collective-permute-done.20 = bf16[48,384]{1,0:T(8,128)(2,1)S(1)} collective-permute-done((bf16[48,384]{1,0:T(8,128)(2,1)S(1)}, bf16[48,384]{1,0:T(8,128)(2,1)S(1)}, u32[]{:S(2)}, u32[]{:S(2)}) %collective-permute-start.20) | collective-permute-done | bytes 36896 | tf_op jit(solution)/shard_map/ppermute | solution.py:101
  174.8 3.4 %collective-permute-done.13 = bf16[48,1152]{1,0:T(8,128)(2,1)S(1)} collective-permute-done((bf16[48,1152]{1,0:T(8,128)(2,1)S(1)}, bf16[48,1152]{1,0:T(8,128)(2,1)S(1)}, u32[]{:S(2)}, u32[]{:S(2)}) %collective-permute-start.13) | collective-permute-done | bytes 110624 | tf_op jit(solution)/shard_map/ppermute | solution.py:101
  184.5 7.5 %collective-permute-start.22 = (bf16[48,3072]{1,0:T(8,128)(2,1)S(1)}, bf16[48,3072]{1,0:T(8,128)(2,1)S(1)}, u32[]{:S(2)}, u32[]{:S(2)}) collective-permute-start(bf16[48,3072]{1,0:T(8,128)(2,1)S(1)} %pad_maximum_fusion.8.mine_ref), channel_id=1, source_target_pairs={{0,32},{1,33},{2,34},{3,35},{4,36},{5,37},{6,38},{7,39},{8,40},{9,... | collective-permute-start | bytes 884744 | tf_op jit(solution)/shard_map/ppermute | solution.py:101
  (148 shorter events, 66.9 us)
Async XLA Ops:
  0.6 18.6 %collective-permute-start.2 = (bf16[48,1536]{1,0:T(8,128)(2,1)}, bf16[48,1536]{1,0:T(8,128)(2,1)S(1)}, u32[]{:S(2)}, u32[]{:S(2)}) collective-permute-start(bf16[48,1536]{1,0:T(8,128)(2,1)} %param.18), channel_id=1, source_target_pairs={{0,0},{16,1},{2,2},{18,3},{4,4},{20,5},{6,6},{22,7},{1,8},{17,9},{... | collective-permute-start | bytes 442376 | tf_op jit(solution)/shard_map/ppermute | solution.py:101
  6.7 12.5 %collective-permute-start.3 = (bf16[48,1536]{1,0:T(8,128)(2,1)}, bf16[48,1536]{1,0:T(8,128)(2,1)S(1)}, u32[]{:S(2)}, u32[]{:S(2)}) collective-permute-start(bf16[48,1536]{1,0:T(8,128)(2,1)} %param.18), channel_id=1, source_target_pairs={{1,0},{17,1},{3,2},{19,3},{5,4},{21,5},{7,6},{23,7},{0,8},{16,9},{... | collective-permute-start | bytes 442376 | tf_op jit(solution)/shard_map/ppermute | solution.py:101
  10.3 6.9 %collective-permute-start = (bf16[48,1152]{1,0:T(8,128)(2,1)S(1)}, bf16[48,1152]{1,0:T(8,128)(2,1)S(1)}, u32[]{:S(2)}, u32[]{:S(2)}) collective-permute-start(bf16[48,1152]{1,0:T(8,128)(2,1)S(1)} %pad_maximum_fusion.12), channel_id=1, source_target_pairs={{0,1},{1,0},{2,3},{3,2},{4,5},{5,4},{6,7},{7,6},{8,9},{9,8},{10,11... | collective-permute-start | bytes 331784 | tf_op jit(solution)/shard_map/ppermute | solution.py:101
  13.6 40.9 %collective-permute-start.7 = (bf16[2,64,1536]{2,1,0:T(8,128)(2,1)}, bf16[2,64,1536]{2,1,0:T(8,128)(2,1)}, u32[]{:S(2)}, u32[]{:S(2)}) collective-permute-start(bf16[2,64,1536]{2,1,0:T(8,128)(2,1)} %get-tuple-element.91), channel_id=1, source_target_pairs={{0,64},{1,65},{2,66},{3,67},{4,68},{5,69},{6,70},{7,71},{8,72},{9,... | collective-permute-start | bytes 1179656 | tf_op jit(solution)/shard_map/ppermute | solution.py:101
  16.3 38.3 %collective-permute-start.8 = (bf16[2,64,1536]{2,1,0:T(8,128)(2,1)}, bf16[2,64,1536]{2,1,0:T(8,128)(2,1)}, u32[]{:S(2)}, u32[]{:S(2)}) collective-permute-start(bf16[2,64,1536]{2,1,0:T(8,128)(2,1)} %get-tuple-element.90), channel_id=1, source_target_pairs={{0,96},{1,97},{2,98},{3,99},{4,100},{5,101},{6,102},{7,103},{8,104... | collective-permute-start | bytes 1179656 | tf_op jit(solution)/shard_map/ppermute | solution.py:101
  17.3 21.0 %collective-permute-start.1 = (bf16[2,2,64,512]{3,2,1,0:T(8,128)(2,1)S(1)}, bf16[2,2,64,512]{3,2,1,0:T(8,128)(2,1)S(1)}, u32[]{:S(2)}, u32[]{:S(2)}) collective-permute-start(bf16[2,2,64,512]{3,2,1,0:T(8,128)(2,1)S(1)} %bitcast.135), channel_id=1, source_target_pairs={{0,1},{1,2},{2,3},{3,4},{4,5},{5,6},{6,7},{7,8},{8,9},{9,10},{10,1... | collective-permute-start | bytes 786440 | tf_op jit(solution)/shard_map/ppermute | solution.py:101
  20.8 25.8 %all-to-all-start = ((bf16[4,2,48,2688]{3,2,1,0:T(8,128)(2,1)}), bf16[4,2,48,2688]{3,2,1,0:T(8,128)(2,1)S(1)}, u32[]{:S(2)}, u32[]{:S(2)}) async-start(bf16[4,2,48,2688]{3,2,1,0:T(8,128)(2,1)} %broadcast_in_dim.35), calls=%async_computation | async-start | bytes 4128768 | tf_op jit(solution)/shard_map/all_to_all | solution.py:105
  36.6 18.0 %collective-permute-start.6 = (bf16[2,64,1536]{2,1,0:T(8,128)(2,1)}, bf16[2,64,1536]{2,1,0:T(8,128)(2,1)}, u32[]{:S(2)}, u32[]{:S(2)}) collective-permute-start(bf16[2,64,1536]{2,1,0:T(8,128)(2,1)} %get-tuple-element.58), channel_id=1, source_target_pairs={{0,32},{1,33},{2,34},{3,35},{4,36},{5,37},{6,38},{7,39},{8,40},{9,... | collective-permute-start | bytes 1179656 | tf_op jit(solution)/shard_map/ppermute | solution.py:101
  41.6 13.0 %collective-permute-start.4 = (bf16[256,512]{1,0:T(8,128)(2,1)S(1)}, bf16[256,512]{1,0:T(8,128)(2,1)S(1)}, u32[]{:S(2)}, u32[]{:S(2)}) collective-permute-start(bf16[256,512]{1,0:T(8,128)(2,1)S(1)} %fusion.3), channel_id=1, source_target_pairs={{0,1},{1,0},{2,3},{3,2},{4,5},{5,4},{6,7},{7,6},{8,9},{9,8},{10,11... | collective-permute-start | bytes 786440 | tf_op jit(solution)/shard_map/ppermute | solution.py:101
  49.4 27.8 %all-to-all-start.1 = ((bf16[4,384,1152]{2,1,0:T(8,128)(2,1)}), bf16[4,384,1152]{2,1,0:T(8,128)(2,1)}, u32[]{:S(2)}, u32[]{:S(2)}) async-start(bf16[4,384,1152]{2,1,0:T(8,128)(2,1)} %get-tuple-element.55), calls=%async_computation.1 | async-start | bytes 7077888 | tf_op jit(solution)/shard_map/all_to_all | solution.py:105
  56.5 18.8 %collective-permute-start.9 = (bf16[256,1536]{1,0:T(8,128)(2,1)S(1)}, bf16[256,1536]{1,0:T(8,128)(2,1)}, u32[]{:S(2)}, u32[]{:S(2)}) collective-permute-start(bf16[256,1536]{1,0:T(8,128)(2,1)S(1)} %bitcast_select_fusion), channel_id=1, source_target_pairs={{0,1},{1,0},{2,3},{3,2},{4,5},{5,4},{6,7},{7,6},{8,9},{9,8},{10,11... | collective-permute-start | bytes 2359304 | tf_op jit(solution)/shard_map/ppermute | solution.py:101
  80.5 8.5 %collective-permute-start.10 = (bf16[2,256,1536]{2,1,0:T(8,128)(2,1)}, bf16[2,256,1536]{2,1,0:T(8,128)(2,1)}, u32[]{:S(2)}, u32[]{:S(2)}) collective-permute-start(bf16[2,256,1536]{2,1,0:T(8,128)(2,1)} %pad_maximum_fusion.1), channel_id=1, source_target_pairs={{0,32},{1,33},{2,34},{3,35},{4,36},{5,37},{6,38},{7,39},{8,40},{9,... | collective-permute-start | bytes 4718600 | tf_op jit(solution)/shard_map/ppermute | solution.py:101
  108.1 6.8 %collective-permute-start.11 = (bf16[512,1536]{1,0:T(8,128)(2,1)S(1)}, bf16[512,1536]{1,0:T(8,128)(2,1)}, u32[]{:S(2)}, u32[]{:S(2)}) collective-permute-start(bf16[512,1536]{1,0:T(8,128)(2,1)S(1)} %shard_map.161), channel_id=1, source_target_pairs={{0,32},{1,33},{2,34},{3,35},{4,36},{5,37},{6,38},{7,39},{8,40},{9,... | collective-permute-start | bytes 4718600 | tf_op jit(solution)/shard_map/ppermute | solution.py:101
  108.2 35.3 %all-to-all-start.2 = ((bf16[4,384,1536]{2,1,0:T(8,128)(2,1)}), bf16[4,384,1536]{2,1,0:T(8,128)(2,1)}, u32[]{:S(2)}, u32[]{:S(2)}) async-start(bf16[4,384,1536]{2,1,0:T(8,128)(2,1)} %shard_map.160), calls=%async_computation.2 | async-start | bytes 9437184 | tf_op jit(solution)/shard_map/all_to_all | solution.py:105
  118.2 19.2 %collective-permute-start.12 = (bf16[256,1536]{1,0:T(8,128)(2,1)}, bf16[256,1536]{1,0:T(8,128)(2,1)}, u32[]{:S(2)}, u32[]{:S(2)}) collective-permute-start(bf16[256,1536]{1,0:T(8,128)(2,1)} %dynamic-slice_bitcast_fusion), channel_id=1, source_target_pairs={{0,1},{1,0},{2,3},{3,2},{4,5},{5,4},{6,7},{7,6},{8,9},{9,8},{10,11... | collective-permute-start | bytes 2359304 | tf_op jit(solution)/shard_map/ppermute | solution.py:101
  147.9 14.3 %all-to-all-start.3 = ((bf16[4,96,1536]{2,1,0:T(8,128)(2,1)}), bf16[4,96,1536]{2,1,0:T(8,128)(2,1)S(1)}, u32[]{:S(2)}, u32[]{:S(2)}) async-start(bf16[4,96,1536]{2,1,0:T(8,128)(2,1)} %bitcast.49), calls=%async_computation.3 | async-start | bytes 2359296 | tf_op jit(solution)/shard_map/all_to_all | solution.py:105
  152.1 30.7 %collective-permute-start.16 = (bf16[2,64,1536]{2,1,0:T(8,128)(2,1)S(1)}, bf16[2,64,1536]{2,1,0:T(8,128)(2,1)S(1)}, u32[]{:S(2)}, u32[]{:S(2)}) collective-permute-start(bf16[2,64,1536]{2,1,0:T(8,128)(2,1)S(1)} %get-tuple-element.98.rest_0_), channel_id=1, source_target_pairs={{0,32},{1,33},{2,34},{3,35},{4,36},{5,37},{6,38},{7,39},{8,40},{9,... | collective-permute-start | bytes 1179656 | tf_op jit(solution)/shard_map/ppermute | solution.py:101
  154.7 28.1 %collective-permute-start.18 = (bf16[2,64,1536]{2,1,0:T(8,128)(2,1)S(1)}, bf16[2,64,1536]{2,1,0:T(8,128)(2,1)S(1)}, u32[]{:S(2)}, u32[]{:S(2)}) collective-permute-start(bf16[2,64,1536]{2,1,0:T(8,128)(2,1)S(1)} %get-tuple-element.100.rest_2_), channel_id=1, source_target_pairs={{0,96},{1,97},{2,98},{3,99},{4,100},{5,101},{6,102},{7,103},{8,104... | collective-permute-start | bytes 1179656 | tf_op jit(solution)/shard_map/ppermute | solution.py:101
  157.3 25.5 %collective-permute-start.17 = (bf16[2,64,1536]{2,1,0:T(8,128)(2,1)S(1)}, bf16[2,64,1536]{2,1,0:T(8,128)(2,1)}, u32[]{:S(2)}, u32[]{:S(2)}) collective-permute-start(bf16[2,64,1536]{2,1,0:T(8,128)(2,1)S(1)} %get-tuple-element.99.rest_1_), channel_id=1, source_target_pairs={{0,64},{1,65},{2,66},{3,67},{4,68},{5,69},{6,70},{7,71},{8,72},{9,... | collective-permute-start | bytes 1179656 | tf_op jit(solution)/shard_map/ppermute | solution.py:101
  162.5 6.6 %collective-permute-start.19 = (bf16[48,384]{1,0:T(8,128)(2,1)S(1)}, bf16[48,384]{1,0:T(8,128)(2,1)S(1)}, u32[]{:S(2)}, u32[]{:S(2)}) collective-permute-start(bf16[48,384]{1,0:T(8,128)(2,1)S(1)} %get-tuple-element.124), channel_id=1, source_target_pairs={{0,0},{1,16},{2,1},{3,17},{4,32},{5,48},{6,33},{7,49},{8,2},{9,18}... | collective-permute-start | bytes 110600 | tf_op jit(solution)/shard_map/ppermute | solution.py:101
  166.7 8.1 %collective-permute-start.20 = (bf16[48,384]{1,0:T(8,128)(2,1)S(1)}, bf16[48,384]{1,0:T(8,128)(2,1)S(1)}, u32[]{:S(2)}, u32[]{:S(2)}) collective-permute-start(bf16[48,384]{1,0:T(8,128)(2,1)S(1)} %get-tuple-element.125), channel_id=1, source_target_pairs={{0,1},{1,17},{2,0},{3,16},{4,33},{5,49},{6,32},{7,48},{8,3},{9,19}... | collective-permute-start | bytes 110600 | tf_op jit(solution)/shard_map/ppermute | solution.py:101
  169.1 9.1 %collective-permute-start.13 = (bf16[48,1152]{1,0:T(8,128)(2,1)S(1)}, bf16[48,1152]{1,0:T(8,128)(2,1)S(1)}, u32[]{:S(2)}, u32[]{:S(2)}) collective-permute-start(bf16[48,1152]{1,0:T(8,128)(2,1)S(1)} %get-tuple-element.112), channel_id=1, source_target_pairs={{0,64},{1,65},{2,66},{3,67},{4,68},{5,69},{6,70},{7,71},{8,72},{9,... | collective-permute-start | bytes 331784 | tf_op jit(solution)/shard_map/ppermute | solution.py:101
  179.6 4.8 %collective-permute-start.21 = (bf16[48,768]{1,0:T(8,128)(2,1)S(1)}, bf16[48,768]{1,0:T(8,128)(2,1)S(1)}, u32[]{:S(2)}, u32[]{:S(2)}) collective-permute-start(bf16[48,768]{1,0:T(8,128)(2,1)S(1)} %pad_maximum_fusion.13), channel_id=1, source_target_pairs={{0,64},{1,65},{2,66},{3,67},{4,68},{5,69},{6,70},{7,71},{8,72},{9,... | collective-permute-start | bytes 221192 | tf_op jit(solution)/shard_map/ppermute | solution.py:101
  184.5 8.9 %collective-permute-start.22 = (bf16[48,3072]{1,0:T(8,128)(2,1)S(1)}, bf16[48,3072]{1,0:T(8,128)(2,1)S(1)}, u32[]{:S(2)}, u32[]{:S(2)}) collective-permute-start(bf16[48,3072]{1,0:T(8,128)(2,1)S(1)} %pad_maximum_fusion.8.mine_ref), channel_id=1, source_target_pairs={{0,32},{1,33},{2,34},{3,35},{4,36},{5,37},{6,38},{7,39},{8,40},{9,... | collective-permute-start | bytes 884744 | tf_op jit(solution)/shard_map/ppermute | solution.py:101
  (21 other events, 111.5 us)
